TPU v7x, 512 devices: a whole 4x4x16 slice. The times are simulated.
512 devices in a mesh: ha: 16 (over y, x), wa: 16 (over z), col: 2 (over core).
Axes of the slice: x: 4, y: 4, z: 16, core: 2. Of those that a mesh axis runs over, the one named last changes fastest.
Arguments:
- inputs: bfloat16 [2, 12, 16, 24576], P('col', None, 'ha', 'wa'), may hold values from -6 to 6
- carried: bfloat16 [2, 2, 16, 24576], P('col', None, 'ha', 'wa'), may hold values from -6 to 6
- gain: float32 [192], replicated, may hold values from 0.1 to 1.9
- weight: bfloat16 [27, 36864], replicated, may hold values from -0.078125 to 0.078125
- cotangent: bfloat16 [2, 12, 32, 49152], P('col', None, 'ha', 'wa'), may hold values from -4 to 4
Outputs:
- grad_inputs: bfloat16 [2, 12, 16, 24576], P('col', None, 'ha', 'wa')
- grad_weight: float32 [2, 27, 18432], P('col', None, ('ha', 'wa'))
- grad_gain: float32 [192], replicated
All inputs are finite; a program needn't handle non-finite values.
Results may differ from a plain program's by a relative error of at most 0.0017.
Values may be sent and summed in bfloat16 or wider, within the bound.
A program may use at most 64 MiB of HBM per device.

v0:
```python
import jax
import jax.numpy as jnp
from jax import lax
from jax.sharding import PartitionSpec as P

CH = 192


def extended(block, sides, width):
    for axis, dim in sides:
        count = lax.axis_size(axis)
        forward = [(i, i + 1) for i in range(count - 1)]
        backward = [(target, source) for source, target in forward]
        low = lax.ppermute(
            lax.slice_in_dim(block, block.shape[dim] - width, None, axis=dim), axis, forward
        )
        high = lax.ppermute(lax.slice_in_dim(block, 0, width, axis=dim), axis, backward)
        block = jnp.concatenate([low, block, high], axis=dim)
    return block


def prepare(inputs, gain):
    values = inputs.astype(jnp.float32)
    scale = lax.rsqrt(jnp.mean(values * values, axis=-1, keepdims=True) + 1e-06)
    normed = values * scale
    act = normed * gain
    activated = jax.nn.silu(act).astype(jnp.bfloat16)
    return (scale, normed, act, activated)


def upsample(field):
    return jnp.repeat(jnp.repeat(field, 2, axis=2), 2, axis=3)


def kernel_terms(upper, cot_flat, frame_count, height, breadth):
    in_channels = upper.shape[-1]
    tap_terms = []
    for t_shift in range(3):
        for h_shift in range(3):
            for w_shift in range(3):
                piece = upper[
                    :,
                    t_shift : t_shift + frame_count,
                    h_shift : h_shift + height,
                    w_shift : w_shift + breadth,
                    :,
                ].reshape(-1, in_channels)
                tap_terms.append(
                    lax.dot_general(
                        piece,
                        cot_flat,
                        (((0,), (0,)), ((), ())),
                        preferred_element_type=jnp.float32,
                    )
                )
    return jnp.stack(tap_terms)


def on_device(inputs, carried, gain, weight, cotangent):
    clip_count, frame_count, coarse_h, merged = inputs.shape
    channels = CH
    coarse_w = merged // channels
    inputs = inputs.reshape(clip_count, frame_count, coarse_h, coarse_w, channels)
    carried = carried.reshape(clip_count, 2, coarse_h, coarse_w, channels)
    cotangent = cotangent.reshape(clip_count, frame_count, 2 * coarse_h, 2 * coarse_w, channels)
    kernel = weight.reshape(3, 3, 3, channels, channels)
    scale, normed, act, activated = prepare(inputs, gain)
    frames = jnp.concatenate([carried, activated], axis=1)
    upper = extended(upsample(frames), (("ha", 2), ("wa", 3)), 1)
    lower = extended(cotangent, (("ha", 2), ("wa", 3)), 1)
    lower = jnp.pad(lower, ((0, 0), (0, 2), (0, 0), (0, 0), (0, 0)))
    height = 2 * coarse_h
    breadth = 2 * coarse_w
    cot_flat = cotangent.reshape(-1, channels)
    half_width = channels // 2 * channels
    groups = lax.axis_size("ha") * lax.axis_size("wa")
    kernel_term = kernel_terms(upper, cot_flat, frame_count, height, breadth)
    blocks = kernel_term.reshape(27, 2, groups, half_width // groups)
    ordered = jnp.transpose(blocks, (2, 1, 0, 3)).reshape(2 * groups, 27, half_width // groups)
    grad_weight = lax.psum_scatter(ordered, ("ha", "wa", "col"), scatter_dimension=0, tiled=True)
    back_field = jnp.zeros(cotangent.shape, jnp.float32)
    for t_shift in range(3):
        for h_shift in range(3):
            for w_shift in range(3):
                source = lower[
                    :,
                    2 - t_shift : 2 - t_shift + frame_count,
                    2 - h_shift : 2 - h_shift + height,
                    2 - w_shift : 2 - w_shift + breadth,
                    :,
                ].reshape(-1, channels)
                product = lax.dot_general(
                    source,
                    kernel[t_shift, h_shift, w_shift],
                    (((1,), (1,)), ((), ())),
                    preferred_element_type=jnp.float32,
                )
                back_field = back_field + product.reshape(cotangent.shape)
    coarse = back_field.reshape(clip_count, frame_count, coarse_h, 2, coarse_w, 2, channels).sum(
        axis=(3, 5)
    )
    sigmoid_act = jax.nn.sigmoid(act)
    grad_act = coarse * sigmoid_act * (1.0 + act * (1.0 - sigmoid_act))
    gain_term = jnp.sum(grad_act * normed, axis=(0, 1, 2, 3))
    grad_gain = lax.psum(gain_term, ("ha", "wa", "col"))
    grad_normed = grad_act * gain
    grad_inputs = scale * (
        grad_normed - normed * jnp.mean(grad_normed * normed, axis=-1, keepdims=True)
    )
    grad_inputs = grad_inputs.astype(jnp.bfloat16).reshape(
        clip_count, frame_count, coarse_h, coarse_w * channels
    )
    return (grad_inputs, grad_weight, grad_gain)


def solution(mesh):
    placed = (
        P("col", None, "ha", "wa"),
        P("col", None, "ha", "wa"),
        P(),
        P(),
        P("col", None, "ha", "wa"),
    )
    return jax.shard_map(
        on_device,
        mesh=mesh,
        in_specs=placed,
        out_specs=(P("col", None, "ha", "wa"), P("col", None, ("ha", "wa")), P()),
        check_vma=False,
    )
```

profile of v0, /device:TPU:6, one launch (start us, length us, event | category | flops | bytes accessed | tf_op | source)
XLA Modules:
  0.0 696.9 jit_solution(6152999202094930721)
XLA Ops:
  10.6 3.4 collective-permute-start.4
  14.0 2.4 collective-permute-start.5
  18.3 5.5 collective-permute-start
  23.8 1.9 collective-permute-start.1
  28.5 1.8 dot_general.260
  33.6 4.3 reshape.469
  40.4 4.4 collective-permute-start.2
  46.2 1.9 fusion.31
  51.8 5.2 collective-permute-start.6
  64.0 1.8 stack.85
  65.8 1.8 stack.91
  67.6 1.8 stack.94
  69.4 1.8 stack.100
  71.2 1.8 stack.103
  73.0 1.8 stack.109
  102.5 1.8 fusion.64
  104.3 1.8 stack.90
  107.1 1.8 stack.92
  108.9 1.9 fusion.67
  110.7 1.8 stack.93
  113.5 1.9 stack.95
  118.0 1.9 fusion.72
  119.9 1.8 stack.98
  122.6 1.8 stack.99
  125.4 1.8 stack.101
  128.2 1.8 stack.102
  132.9 2.0 stack.105
  137.4 1.9 fusion.84
  139.3 1.8 stack.110
  168.6 11.5 %copy.43 = f32[256,2,27,72]{3,1,0,2:T(2,128)} copy(f32[256,2,27,72]{3,0,1,2:T(8,128)} %bitcast.368) | data formatting | bytes 7962624 | tf_op jit(solution)/shard_map/transpose | solution.py:79
  182.1 110.2 %psum.7 = f32[192]{0:T(256)} all-reduce(f32[192]{0:T(256)S(1)} %reduce_sum.60), channel_id=1, replica_groups=mesh['ha'=16,'wa'=16,'col'=2] {'ha','wa','col'}, use_global_device_ids=true, to_apply=%region_7.8 | all-reduce | flops 192 | bytes 1536 | tf_op jit(solution)/shard_map/psum | solution.py:105
  292.3 396.2 %all-reduce.4.cloned.1.call-done = f32[512,27,72]{2,0,1:T(8,128)} async-done(((f32[512,27,72]{2,0,1:T(8,128)}), f32[512,27,72]{2,0,1:T(8,128)}) %all-reduce.4.cloned.1.call-update) | async-done | bytes 3981328
  (189 shorter events, 96.8 us)
Async XLA Ops:
  7.2 681.4 %all-reduce.4.cloned.1.call-start = ((), (), s32[]{:S(2)}) async-start(), calls=%async_computation | async-start | bytes 14155776
  8.2 15.6 %copy-start.17 = (f32[12,8]{1,0:T(8,128)}, f32[12,8]{1,0:T(8,128)S(1)}, u32[]{:S(2)}) copy-start(f32[12,8]{1,0:T(8,128)S(1)} %add_rsqrt_fusion) | copy-start | bytes 1156
  10.6 37.4 %collective-permute-start.4 = (bf16[1,14,1,16,192]{4,3,1,2,0:T(8,128)(2,1)}, bf16[1,14,1,16,192]{4,3,1,2,0:T(8,128)(2,1)S(1)}, u32[]{:S(2)}, u32[]{:S(2)}) collective-permute-start(bf16[1,14,1,16,192]{4,3,1,2,0:T(8,128)(2,1)} %slice.384), channel_id=1, source_target_pairs={{0,32},{32,64},{64,96},{96,128},{128,160},{160,192},{192,224},{224... | collective-permute-start | bytes 258056 | tf_op jit(solution)/shard_map/ppermute | solution.py:14
  14.0 34.0 %collective-permute-start.5 = (bf16[1,14,1,16,192]{4,3,1,2,0:T(8,128)(2,1)}, bf16[1,14,1,16,192]{4,3,1,2,0:T(8,128)(2,1)}, u32[]{:S(2)}, u32[]{:S(2)}) collective-permute-start(bf16[1,14,1,16,192]{4,3,1,2,0:T(8,128)(2,1)} %slice.384), channel_id=1, source_target_pairs={{32,0},{64,32},{96,64},{128,96},{160,128},{192,160},{224,192},{256... | collective-permute-start | bytes 258056 | tf_op jit(solution)/shard_map/ppermute | solution.py:17
  18.3 19.6 %collective-permute-start = (bf16[1,12,1,16,192]{4,3,2,1,0:T(8,128)(2,1)S(1)}, bf16[1,12,1,16,192]{4,3,2,1,0:T(8,128)(2,1)}, u32[]{:S(2)}, u32[]{:S(2)}) collective-permute-start(bf16[1,12,1,16,192]{4,3,2,1,0:T(8,128)(2,1)S(1)} %get-tuple-element.39), channel_id=1, source_target_pairs={{0,32},{32,64},{64,96},{96,128},{128,160},{160,192},{192,224},{224... | collective-permute-start | bytes 221192 | tf_op jit(solution)/shard_map/ppermute | solution.py:14
  23.8 15.0 %collective-permute-start.1 = (bf16[1,12,1,16,192]{4,3,2,1,0:T(8,128)(2,1)}, bf16[1,12,1,16,192]{4,3,2,1,0:T(8,128)(2,1)}, u32[]{:S(2)}, u32[]{:S(2)}) collective-permute-start(bf16[1,12,1,16,192]{4,3,2,1,0:T(8,128)(2,1)} %get-tuple-element.38), channel_id=1, source_target_pairs={{32,0},{64,32},{96,64},{128,96},{160,128},{192,160},{224,192},{256... | collective-permute-start | bytes 221192 | tf_op jit(solution)/shard_map/ppermute | solution.py:17
  40.4 34.4 %collective-permute-start.2 = (bf16[1,12,4,1,192]{4,3,2,1,0:T(2,128)(2,1)}, bf16[1,12,4,1,192]{4,3,2,1,0:T(2,128)(2,1)}, u32[]{:S(2)}, u32[]{:S(2)}) collective-permute-start(bf16[1,12,4,1,192]{4,3,2,1,0:T(2,128)(2,1)} %get-tuple-element.26), channel_id=1, source_target_pairs={{0,2},{2,4},{4,6},{6,8},{8,10},{10,12},{12,14},{14,16},{16,18},{18... | collective-permute-start | bytes 55304 | tf_op jit(solution)/shard_map/ppermute | solution.py:14
  44.9 29.9 %collective-permute-start.3 = (bf16[1,12,4,1,192]{4,3,2,1,0:T(2,128)(2,1)}, bf16[1,12,4,1,192]{4,3,2,1,0:T(2,128)(2,1)}, u32[]{:S(2)}, u32[]{:S(2)}) collective-permute-start(bf16[1,12,4,1,192]{4,3,2,1,0:T(2,128)(2,1)} %get-tuple-element.25), channel_id=1, source_target_pairs={{2,0},{4,2},{6,4},{8,6},{10,8},{12,10},{14,12},{16,14},{18,16},{20... | collective-permute-start | bytes 55304 | tf_op jit(solution)/shard_map/ppermute | solution.py:17
  49.0 1.7 copy-start
  51.8 38.5 %collective-permute-start.6 = (bf16[1,14,4,1,192]{4,3,2,1,0:T(2,128)(2,1)}, bf16[1,14,4,1,192]{4,3,2,1,0:T(2,128)(2,1)}, u32[]{:S(2)}, u32[]{:S(2)}) collective-permute-start(bf16[1,14,4,1,192]{4,3,2,1,0:T(2,128)(2,1)} %get-tuple-element.24), channel_id=1, source_target_pairs={{0,2},{2,4},{4,6},{6,8},{8,10},{10,12},{12,14},{14,16},{16,18},{18... | collective-permute-start | bytes 64520 | tf_op jit(solution)/shard_map/ppermute | solution.py:14
  57.0 33.3 %collective-permute-start.7 = (bf16[1,14,4,1,192]{4,3,2,1,0:T(2,128)(2,1)}, bf16[1,14,4,1,192]{4,3,2,1,0:T(2,128)(2,1)}, u32[]{:S(2)}, u32[]{:S(2)}) collective-permute-start(bf16[1,14,4,1,192]{4,3,2,1,0:T(2,128)(2,1)} %get-tuple-element.23), channel_id=1, source_target_pairs={{2,0},{4,2},{6,4},{8,6},{10,8},{12,10},{14,12},{16,14},{18,16},{20... | collective-permute-start | bytes 64520 | tf_op jit(solution)/shard_map/ppermute | solution.py:17
  78.4 6.0 copy-start.15
  79.1 7.5 %copy-start.1 = (f32[12,2,16,192]{3,2,1,0:T(8,128)S(1)}, f32[12,2,16,192]{3,2,1,0:T(8,128)}, u32[]{:S(2)}) copy-start(f32[12,2,16,192]{3,2,1,0:T(8,128)} %fusion.31) | copy-start | bytes 884740
  104.3 36.8 %copy-start.9 = (f32[1,2,256,72]{3,2,1,0:T(8,128)S(1)}, f32[1,2,256,72]{3,2,1,0:T(8,128)}, u32[]{:S(2)}) copy-start(f32[1,2,256,72]{3,2,1,0:T(8,128)} %stack.85) | copy-start | bytes 442372
  108.9 36.3 %copy-start.3 = (f32[1,2,256,72]{3,2,1,0:T(8,128)S(1)}, f32[1,2,256,72]{3,2,1,0:T(8,128)}, u32[]{:S(2)}) copy-start(f32[1,2,256,72]{3,2,1,0:T(8,128)} %stack.88) | copy-start | bytes 442372
  113.5 35.8 %copy-start.8 = (f32[1,2,256,72]{3,2,1,0:T(8,128)S(1)}, f32[1,2,256,72]{3,2,1,0:T(8,128)}, u32[]{:S(2)}) copy-start(f32[1,2,256,72]{3,2,1,0:T(8,128)} %stack.91) | copy-start | bytes 442372
  118.0 35.4 %copy-start.7 = (f32[1,2,256,72]{3,2,1,0:T(8,128)S(1)}, f32[1,2,256,72]{3,2,1,0:T(8,128)}, u32[]{:S(2)}) copy-start(f32[1,2,256,72]{3,2,1,0:T(8,128)} %stack.94) | copy-start | bytes 442372
  122.6 34.8 %copy-start.2 = (f32[1,2,256,72]{3,2,1,0:T(8,128)S(1)}, f32[1,2,256,72]{3,2,1,0:T(8,128)}, u32[]{:S(2)}) copy-start(f32[1,2,256,72]{3,2,1,0:T(8,128)} %stack.97) | copy-start | bytes 442372
  127.2 33.3 %copy-start.6 = (f32[1,2,256,72]{3,2,1,0:T(8,128)S(1)}, f32[1,2,256,72]{3,2,1,0:T(8,128)}, u32[]{:S(2)}) copy-start(f32[1,2,256,72]{3,2,1,0:T(8,128)} %stack.100) | copy-start | bytes 442372
  130.9 31.8 %copy-start.5 = (f32[1,2,256,72]{3,2,1,0:T(8,128)S(1)}, f32[1,2,256,72]{3,2,1,0:T(8,128)}, u32[]{:S(2)}) copy-start(f32[1,2,256,72]{3,2,1,0:T(8,128)} %stack.103) | copy-start | bytes 442372
  136.3 30.8 %copy-start.4 = (f32[1,2,256,72]{3,2,1,0:T(8,128)S(1)}, f32[1,2,256,72]{3,2,1,0:T(8,128)}, u32[]{:S(2)}) copy-start(f32[1,2,256,72]{3,2,1,0:T(8,128)} %stack.109) | copy-start | bytes 442372
  141.1 18.7 %copy-start.14 = (f32[1,2,256,72]{3,2,1,0:T(8,128)S(1)}, f32[1,2,256,72]{3,2,1,0:T(8,128)}, u32[]{:S(2)}) copy-start(f32[1,2,256,72]{3,2,1,0:T(8,128)} %stack.99) | copy-start | bytes 442372
  141.1 20.2 %copy-start.11 = (f32[1,2,256,72]{3,2,1,0:T(8,128)S(1)}, f32[1,2,256,72]{3,2,1,0:T(8,128)}, u32[]{:S(2)}) copy-start(f32[1,2,256,72]{3,2,1,0:T(8,128)} %stack.101) | copy-start | bytes 442372
  141.1 20.9 %copy-start.13 = (f32[1,2,256,72]{3,2,1,0:T(8,128)S(1)}, f32[1,2,256,72]{3,2,1,0:T(8,128)}, u32[]{:S(2)}) copy-start(f32[1,2,256,72]{3,2,1,0:T(8,128)} %stack.102) | copy-start | bytes 442372
  141.1 23.1 %copy-start.12 = (f32[1,2,256,72]{3,2,1,0:T(8,128)S(1)}, f32[1,2,256,72]{3,2,1,0:T(8,128)}, u32[]{:S(2)}) copy-start(f32[1,2,256,72]{3,2,1,0:T(8,128)} %stack.105) | copy-start | bytes 442372
  141.1 26.7 %copy-start.10 = (f32[1,2,256,72]{3,2,1,0:T(8,128)S(1)}, f32[1,2,256,72]{3,2,1,0:T(8,128)}, u32[]{:S(2)}) copy-start(f32[1,2,256,72]{3,2,1,0:T(8,128)} %stack.110) | copy-start | bytes 442372
  180.1 0.7 copy-start.18
  180.1 0.9 copy-start.20
  180.1 1.1 copy-start.19
  180.1 1.3 copy-start.16
Sparse Core Ops, SparseCore 0:
  180.2 508.3 all-reduce.3
where the time goes:
time: 699 us; the launch traced here: 697 us
  waiting for transfers between devices  396 us (57%)
  blocking collectives  110 us (16%)
  local copies, waits for them, and re-layouts  101 us (14%)
  matrix products  40 us (6%)
  starting transfers between devices  25.6 us (4%)
  between operations  14.8 us (2%)
  other arithmetic  9.33 us (1%)
    unnamed x2, waiting for transfers between devices  396 us
    psum x1, blocking collectives, on_device(): grad_gain = lax.psum(gain_term, ('ha', 'wa', 'col'))  110 us
    another operation x28, local copies, waits for them, and re-layouts, kernel_terms(): return jnp.stack(tap_terms)  39.7 us
    unnamed x71, local copies, waits for them, and re-layouts  30.5 us
    dot_general x27, matrix products, kernel_terms(): lax.dot_general(piece, cot_flat, (((0,), (0,)), ((), ())), preferred_elem...  26.7 us
    ppermute x4, starting transfers between devices, extended(): lax.ppermute(lax.slice_in_dim(block, block.shape[dim] - width, None, axis...  18.5 us
  transfers between devices with their start and end apart: 9, of which 1 were waited for; matrix products, arithmetic and copies ran while one was open for 8% of the time, Pallas kernels for 0%

commit v1 on v0

v1 whole, which is shorter than its diff:
```python
import functools

import jax
import jax.numpy as jnp
from jax import lax
from jax.experimental import pallas as pl
from jax.experimental.pallas import tpu as pltpu
from jax.sharding import PartitionSpec as P

CH = 192
T = 12
S = 8
TP = 16
ROWS = S * TP
HALF = 896
MESH = pl.DeviceIdType.MESH
F32 = jnp.float32
BF16 = jnp.bfloat16
NT = (((1,), (1,)), ((), ()))


def remote(src, dst, send, recv, device):
    return pltpu.make_async_remote_copy(
        src_ref=src, dst_ref=dst, send_sem=send, recv_sem=recv, device_id=device, device_id_type=MESH
    )


def kernel(
    x_ref, car_ref, gain_ref, w_ref, cot_ref,
    gi_ref, gw_ref, gg_ref,
    wv, ws, wte, wto, rws, cs, colh, uf, ut, dk, de, do, p, r1, t2, q2, r2, vs, zb, r3, gh, gz, gc,
    w_sem, halo_s, halo_r, core_s, core_r, s1s, s1r, s2s, s2r, s3s, s3r, ghs, ghr, gzs, gzr, gcs, gcr,
):
    ha = lax.axis_index("ha")
    wa = lax.axis_index("wa")
    col = lax.axis_index("col")
    qy, qx = ha // 4, ha % 4
    up, down = (ha + 15) % 16, (ha + 1) % 16
    left, right = (wa + 15) % 16, (wa + 1) % 16
    other = 1 - col

    barrier = pltpu.get_barrier_semaphore()

    def greet(d, _):
        pl.semaphore_signal(barrier, inc=1, device_id=((ha + d) % 16, wa, col), device_id_type=MESH)
        pl.semaphore_signal(barrier, inc=1, device_id=(ha, (wa + d) % 16, col), device_id_type=MESH)
        return 0

    lax.fori_loop(1, 16, greet, 0)
    pl.semaphore_signal(barrier, inc=1, device_id=(ha, wa, other), device_id_type=MESH)
    for h in (up, down):
        for w in (left, right):
            pl.semaphore_signal(barrier, inc=1, device_id=(h, w, col), device_id_type=MESH)

    w_copy = pltpu.make_async_copy(w_ref, wv, w_sem)
    w_copy.start()

    pad4 = jnp.zeros((TP - T, 2 * S * CH), F32)
    for row in range(2):
        value = cot_ref[:, row, :].astype(F32)
        value = jnp.concatenate([value, pad4], axis=0).astype(BF16)
        rws[1 + row] = value
        cs[0, row, :, 0:CH] = value[:, 0:CH]
        cs[1, row, :, 0:CH] = value[:, 15 * CH : 16 * CH]

    pl.semaphore_wait(barrier, 35)

    halos = []

    def halo(src, dst, device):
        n = len(halos)
        copy = remote(src, dst, halo_s.at[n], halo_r.at[n], device)
        copy.start()
        halos.append(copy)

    halo(rws.at[1], rws.at[3], (up, wa, col))
    halo(rws.at[2], rws.at[0], (down, wa, col))
    halo(cs.at[0], colh.at[1, pl.ds(1, 2)], (ha, left, col))
    halo(cs.at[1], colh.at[0, pl.ds(1, 2)], (ha, right, col))
    halo(cs.at[0, 0], colh.at[1, 3], (up, left, col))
    halo(cs.at[1, 0], colh.at[0, 3], (up, right, col))
    halo(cs.at[0, 1], colh.at[1, 0], (down, left, col))
    halo(cs.at[1, 1], colh.at[0, 0], (down, right, col))

    gain = gain_ref[...]
    pad = jnp.zeros((TP - T, CH), F32)
    x = jnp.concatenate(
        [piece for s in range(S) for piece in (x_ref[:, s * CH : (s + 1) * CH].astype(F32), pad)], axis=0
    )
    scale = lax.rsqrt(jnp.mean(x * x, axis=-1, keepdims=True) + 1e-06)
    normed = x * scale
    act = normed * gain
    sig = 1.0 / (1.0 + jnp.exp(-act))
    activated = (act * sig).astype(BF16).astype(F32).reshape(S, TP, CH)
    for s in range(S):
        uf[s, 0:2, :] = car_ref[:, s * CH : (s + 1) * CH].astype(F32)
        uf[s, 2 : 2 + TP, :] = activated[s]

    m = lax.broadcasted_iota(jnp.int32, (CH, CH), 0)
    lane = lax.broadcasted_iota(jnp.int32, (CH, CH), 1)
    mm = jnp.where(m >= 96, m - 96, m)
    first = (mm >= 24).astype(jnp.int32) + (mm >= 48).astype(jnp.int32) + (mm >= 72).astype(jnp.int32)
    rest = mm - 24 * first
    second = (rest >= 6).astype(jnp.int32) + (rest >= 12).astype(jnp.int32) + (rest >= 18).astype(jnp.int32)
    swapped = 24 * second + 6 * first + (rest - 6 * second)
    channel = jnp.where(m >= 96, swapped, mm)
    for k, half in ((0, col), (1, other)):
        sel = (lane == channel + 96 * half).astype(F32).astype(BF16)
        for a in range(3):
            u = uf[:, a : a + TP, :].reshape(ROWS, CH).astype(BF16)
            ut[2 * k, a] = lax.dot_general(sel, u, NT, preferred_element_type=F32).astype(BF16)
    u_copy = remote(ut.at[2], ut.at[1], core_s.at[0], core_r.at[0], (ha, wa, other))
    u_copy.start()

    for copy in halos:
        copy.wait_recv()
    top = (ha > 0).astype(F32)
    bottom = (ha < 15).astype(F32)
    at_left = (wa > 0).astype(F32)
    at_right = (wa < 15).astype(F32)
    zero64 = jnp.zeros((TP, 64), BF16)
    dk[0 : 2 * ROWS, 9 * CH :] = jnp.zeros((2 * ROWS, 2 * HALF - 9 * CH), BF16)
    for b in range(3):
        lo_row, hi_row = ((2, 3), (1, 2), (0, 1))[b]

        def rows_of(load):
            one, two = load(lo_row).astype(F32), load(hi_row).astype(F32)
            if b == 0:
                two = two * bottom
            if b == 2:
                one = one * top
            return one + two

        cols = {}
        for j in range(2 * S):
            cols[j] = rows_of(lambda r: rws[r, :, j * CH : (j + 1) * CH])
        cols[-1] = rows_of(lambda r: colh[0, r, :, 0:CH]) * at_left
        cols[2 * S] = rows_of(lambda r: colh[1, r, :, 0:CH]) * at_right
        for e in range(3):
            be = 3 * b + e
            for s in range(S):
                j = 2 * s + 1 - e
                d = cols[j] + cols[j + 1]
                high = d.astype(BF16)
                low = (d - high.astype(F32)).astype(BF16)
                for k, part in ((0, high), (1, low)):
                    at = k * ROWS + s * TP
                    dk[at : at + TP, be * CH : (be + 1) * CH] = part
                    de[at : at + TP, be * 256 : (be + 1) * 256] = jnp.concatenate([part, zero64], axis=1)
                    do[at : at + TP, be * 256 : (be + 1) * 256] = jnp.concatenate([zero64, part], axis=1)
    d_copies = []
    for hf in range(2):
        lanes = pl.ds(hf * HALF, HALF)
        copy = remote(
            dk.at[pl.ds(0, 2 * ROWS), lanes], dk.at[pl.ds(2 * ROWS, 2 * ROWS), lanes],
            core_s.at[1 + hf], core_r.at[1 + hf], (ha, wa, other),
        )
        copy.start()
        d_copies.append(copy)

    w_copy.wait()

    def widen(n, _):
        lanes = pl.ds(pl.multiple_of(n * 128, 128), 128)
        for t8 in range(4):
            count = 8 if t8 < 3 else 3
            at = pl.multiple_of((t8 * 288 + n) * 8, 8)
            ws[pl.ds(at, count), :] = wv[t8 * 8 : t8 * 8 + count, lanes].astype(F32)
        return 0

    lax.fori_loop(0, 288, widen, 0, unroll=8)
    for a in range(3):
        wte[a * 128 + 96 : (a + 1) * 128, :] = jnp.zeros((32, 9 * 256), BF16)
        wto[a * 128 + 96 : (a + 1) * 128, :] = jnp.zeros((32, 9 * 256), BF16)
        for be in range(9):
            t8, tr = (9 * a + be) // 8, (9 * a + be) % 8
            tiles = [ws[pl.ds((t8 * 288 + j) * 8 + tr, 96, stride=24), :].astype(BF16) for j in range(3)]
            rows = slice(a * 128, a * 128 + 96)
            wte[rows, be * 256 : be * 256 + 128] = tiles[0]
            wte[rows, be * 256 + 128 : be * 256 + 256] = tiles[1]
            wto[rows, be * 256 : be * 256 + 128] = tiles[1]
            wto[rows, be * 256 + 128 : be * 256 + 256] = tiles[2]

    def ring(hf, d):
        if hf == 0:
            return ((qy + d) % 4) * 4 + qx
        return qy * 4 + (qx + d) % 4

    mine = (qy, qx)
    u_copy.wait_recv()
    ones = {}
    for hf in range(2):
        d_copies[hf].wait_recv()
        for a in range(3):
            rows = slice(hf * 96, hf * 96 + 96)
            own, his = ut[0, a, rows, :], ut[1, a, rows, :]
            lhs = jnp.concatenate([own, own, his, his], axis=1)
            part = jnp.dot(lhs, dk[:, hf * HALF : (hf + 1) * HALF], preferred_element_type=F32)
            p[a, hf] = part.reshape(4, 24, HALF)
            for d in range(1, 4):
                copy = remote(
                    p.at[a, hf, (mine[hf] + d) % 4], r1.at[a, hf, d - 1], s1s.at[a, hf, d - 1], s1r.at[a, hf, d - 1],
                    (ring(hf, d), wa, col),
                )
                copy.start()
                ones[a, hf, d] = copy

    coarse = None
    pair = lax.broadcasted_iota(jnp.int32, (128, CH), 0)
    chan = lax.broadcasted_iota(jnp.int32, (128, CH), 1)
    for parity, (lhs_ref, rhs_ref) in enumerate(((de, wte), (do, wto))):
        g = lax.dot_general(lhs_ref[...], rhs_ref[...], NT, preferred_element_type=F32)
        g = g[0:ROWS] + g[ROWS : 2 * ROWS]
        g = (
            g[:, 256:384]
            + pltpu.roll(g[:, 128:256], ROWS - 1, axis=0)
            + pltpu.roll(g[:, 0:128], ROWS - 2, axis=0)
        )
        spread = (chan == 2 * pair + parity).astype(F32)
        g = jnp.dot(g, spread, precision=lax.Precision.HIGHEST, preferred_element_type=F32)
        coarse = g if coarse is None else coarse + g
    grad_act = coarse * (sig * (1.0 + act * (1.0 - sig)))
    gain_term = jnp.sum(grad_act * normed, axis=0, keepdims=True)
    gh[ha] = jnp.concatenate([gain_term, jnp.zeros((1, 64), F32)], axis=1)
    gh_copies = []

    def gh_send(d, _):
        remote(gh.at[ha], gh.at[ha], ghs.at[d - 1], ghr.at[d - 1], ((ha + d) % 16, wa, col)).start()
        return 0

    lax.fori_loop(1, 16, gh_send, 0)
    grad_normed = grad_act * gain
    grad_in = scale * (grad_normed - normed * jnp.mean(grad_normed * normed, axis=-1, keepdims=True))
    for s in range(S):
        gi_ref[:, s * CH : (s + 1) * CH] = grad_in[s * TP : s * TP + T].astype(BF16)

    twos = {}
    for a in range(3):
        for hf in range(2):
            for d in range(1, 4):
                ones[a, hf, d].wait_recv()
            total = p[a, hf, mine[hf]] + r1[a, hf, 0] + r1[a, hf, 1] + r1[a, hf, 2]
            t2[0:24, :] = total
            t2[24:32, :] = jnp.zeros((8, HALF), F32)
            for k in range(4):
                q2[a, hf, k] = t2[6 * k : 6 * k + 8, :]
            for d in range(1, 4):
                copy = remote(
                    q2.at[a, hf, (mine[1 - hf] + d) % 4], r2.at[a, hf, d - 1], s2s.at[a, hf, d - 1],
                    s2r.at[a, hf, d - 1], (ring(1 - hf, d), wa, col),
                )
                copy.start()
                twos[a, hf, d] = copy

    def gh_wait(d, _):
        src = (ha + 16 - d) % 16
        remote(gh.at[ha], gh.at[src], ghs.at[d - 1], ghr.at[d - 1], (src, wa, col)).wait_recv()
        return 0

    lax.fori_loop(1, 16, gh_wait, 0)
    gz[wa] = jnp.sum(gh[...], axis=0)

    def gz_send(d, _):
        remote(gz.at[wa], gz.at[wa], gzs.at[d - 1], gzr.at[d - 1], (ha, (wa + d) % 16, col)).start()
        return 0

    lax.fori_loop(1, 16, gz_send, 0)

    for a in range(3):
        for hf in range(2):
            for d in range(1, 4):
                twos[a, hf, d].wait_recv()
            total = q2[a, hf, mine[1 - hf]] + r2[a, hf, 0] + r2[a, hf, 1] + r2[a, hf, 2]
            for k in range(7):
                at = (7 * hf + k) * 8
                vs[a, at : at + 8, :] = total[:, k * 128 : (k + 1) * 128]
        vs[a, 112:192, :] = jnp.zeros((80, 128), F32)
        y = []
        for i in range(6):
            tiles = jnp.concatenate([vs[a, pl.ds(j * 8 + i, 8, stride=24), :] for j in range(3)], axis=1)
            y.append((tiles[:, 0:CH], tiles[:, CH : 2 * CH]))
        for w in range(16):
            i0, o0 = (72 * w) // CH, (72 * w) % CH
            n0 = min(72, CH - o0)
            pieces = []
            for parity in range(2):
                pieces.append(y[i0][parity][:, o0 : o0 + n0])
                if n0 < 72:
                    pieces.append(y[i0 + 1][parity][:, 0 : 72 - n0])
            tile = jnp.concatenate(pieces, axis=1)
            zb[a, w] = tile[:, 0:128]
            spare = jnp.concatenate([tile[k : k + 1, 128:144] for k in range(4)], axis=1)
            zb[a, w, 5:6, 0:64] = spare

        def z_send(d, _):
            remote(
                zb.at[a, (wa + d) % 16], r3.at[a, d - 1], s3s.at[a, d - 1], s3r.at[a, d - 1],
                (ha, (wa + d) % 16, col),
            ).start()
            return 0

        lax.fori_loop(1, 16, z_send, 0)

    def gz_wait(d, _):
        src = (wa + 16 - d) % 16
        remote(gz.at[wa], gz.at[src], gzs.at[d - 1], gzr.at[d - 1], (ha, src, col)).wait_recv()
        return 0

    lax.fori_loop(1, 16, gz_wait, 0)
    gc[0] = jnp.sum(gz[...], axis=0)
    gc_copy = remote(gc.at[0], gc.at[1], gcs, gcr, (ha, wa, other))
    gc_copy.start()

    for a in range(3):

        def z_wait(d, _):
            remote(
                zb.at[a, (wa + d) % 16], r3.at[a, d - 1], s3s.at[a, d - 1], s3r.at[a, d - 1],
                (ha, (wa + d) % 16, col),
            ).wait()
            return 0

        lax.fori_loop(1, 16, z_wait, 0)
        total = zb[a, wa] + jnp.sum(r3[a], axis=0)
        for be in range(9):
            k = be // 2
            if be % 2 == 0:
                row = total[k : k + 1, 0:72]
            else:
                row = jnp.concatenate([total[k : k + 1, 72:128], total[5:6, 16 * k : 16 * k + 16]], axis=1)
            gw_ref[9 * a + be : 9 * a + be + 1, :] = row

    gc_copy.wait()
    gg_ref[...] = (gc[0] + gc[1])[:, 0:CH]

    for copy in halos + d_copies + [u_copy] + list(ones.values()) + list(twos.values()):
        copy.wait_send()

    def g_done(d, _):
        remote(gh.at[ha], gh.at[ha], ghs.at[d - 1], ghr.at[d - 1], ((ha + d) % 16, wa, col)).wait_send()
        remote(gz.at[wa], gz.at[wa], gzs.at[d - 1], gzr.at[d - 1], (ha, (wa + d) % 16, col)).wait_send()
        return 0

    lax.fori_loop(1, 16, g_done, 0)


def on_device(inputs, carried, gain, weight, cotangent):
    vmem = pl.BlockSpec(memory_space=pltpu.VMEM)
    dma = pltpu.SemaphoreType.DMA
    gi, gw, gg = pl.pallas_call(
        kernel,
        out_shape=(
            jax.ShapeDtypeStruct((T, S * CH), BF16),
            jax.ShapeDtypeStruct((27, 72), F32),
            jax.ShapeDtypeStruct((1, CH), F32),
        ),
        in_specs=[vmem, vmem, vmem, pl.BlockSpec(memory_space=pl.ANY), vmem],
        out_specs=(vmem, vmem, vmem),
        scratch_shapes=[
            pltpu.VMEM((27, CH * CH), BF16),
            pltpu.VMEM((4 * 288 * 8, 128), F32),
            pltpu.VMEM((384, 9 * 256), BF16),
            pltpu.VMEM((384, 9 * 256), BF16),
            pltpu.VMEM((4, TP, 2 * S * CH), BF16),
            pltpu.VMEM((2, 2, TP, 256), BF16),
            pltpu.VMEM((2, 4, TP, 256), BF16),
            pltpu.VMEM((S, 24, CH), F32),
            pltpu.VMEM((3, 3, CH, ROWS), BF16),
            pltpu.VMEM((4 * ROWS, 2 * HALF), BF16),
            pltpu.VMEM((2 * ROWS, 9 * 256), BF16),
            pltpu.VMEM((2 * ROWS, 9 * 256), BF16),
            pltpu.VMEM((3, 2, 4, 24, HALF), F32),
            pltpu.VMEM((3, 2, 3, 24, HALF), F32),
            pltpu.VMEM((32, HALF), F32),
            pltpu.VMEM((3, 2, 4, 8, HALF), F32),
            pltpu.VMEM((3, 2, 3, 8, HALF), F32),
            pltpu.VMEM((3, 192, 128), F32),
            pltpu.VMEM((3, 16, 8, 128), F32),
            pltpu.VMEM((3, 15, 8, 128), F32),
            pltpu.VMEM((16, 1, 256), F32),
            pltpu.VMEM((16, 1, 256), F32),
            pltpu.VMEM((2, 1, 256), F32),
            dma(()), dma((8,)), dma((8,)), dma((3,)), dma((3,)),
            dma((3, 2, 3)), dma((3, 2, 3)), dma((3, 2, 3)), dma((3, 2, 3)),
            dma((3, 15)), dma((3, 15)), dma((15,)), dma((15,)), dma((15,)), dma((15,)), dma(()), dma(()),
        ],
        compiler_params=pltpu.CompilerParams(
            collective_id=0, has_side_effects=True, vmem_limit_bytes=50 * 1024 * 1024
        ),
    )(
        inputs.reshape(T, S * CH),
        carried.reshape(2, S * CH),
        gain.reshape(1, CH),
        weight,
        cotangent.reshape(T, 2, 2 * S * CH),
    )
    return gi.reshape(inputs.shape), gw.reshape(1, 27, 72), gg.reshape(CH)


def solution(mesh):
    placed = (
        P("col", None, "ha", "wa"),
        P("col", None, "ha", "wa"),
        P(),
        P(),
        P("col", None, "ha", "wa"),
    )
    return jax.shard_map(
        on_device,
        mesh=mesh,
        in_specs=placed,
        out_specs=(P("col", None, "ha", "wa"), P("col", None, ("ha", "wa")), P()),
        check_vma=False,
    )
```

time: 699 us -> 67 us (0.10)
  the two profiles are of different devices: /device:TPU:6 before, /device:TPU:1 now
where the time goes in v1:
time: 67 us; the launch traced here: 66.7 us
  Pallas kernels  59.6 us (89%)
  local copies, waits for them, and re-layouts  6.53 us (10%)
    pallas_call x1, Pallas kernels, on_device(): pl.pallas_call(kernel, out_shape=(jax.ShapeDtypeStruct((T, S * CH), BF16)...  59.6 us
    unnamed x13, local copies, waits for them, and re-layouts  6.53 us

profile of v1, /device:TPU:1, one launch (start us, length us, event | category | flops | bytes accessed | tf_op | source)
XLA Modules:
  0.0 66.7 jit_solution(17368375871440765475)
XLA Ops:
  0.6 0.0 copy-start
  0.6 1.7 %copy-done = bf16[27,36864]{1,0:T(8,128)(2,1)S(1)} copy-done((bf16[27,36864]{1,0:T(8,128)(2,1)S(1)}, bf16[27,36864]{1,0:T(8,128)(2,1)}, u32[]{:S(2)}) %copy-start) | copy-done | bytes 1990680
  2.3 0.0 copy-start.1
  2.3 0.9 %copy-done.1 = bf16[1,12,2,3072]{3,2,1,0:T(2,128)(2,1)S(1)} copy-done((bf16[1,12,2,3072]{3,2,1,0:T(2,128)(2,1)S(1)}, bf16[1,12,2,3072]{3,2,1,0:T(2,128)(2,1)}, u32[]{:S(2)}) %copy-start.1) | copy-done | bytes 147480
  3.2 0.0 copy-start.2
  3.2 0.8 %copy-done.2 = bf16[1,12,1,1536]{3,1,2,0:T(8,128)(2,1)S(1)} copy-done((bf16[1,12,1,1536]{3,1,2,0:T(8,128)(2,1)S(1)}, bf16[1,12,1,1536]{3,1,2,0:T(8,128)(2,1)}, u32[]{:S(2)}) %copy-start.2) | copy-done | bytes 36888
  4.0 0.0 copy-start.3
  4.0 0.7 %copy-done.3 = bf16[1,2,1,1536]{3,1,2,0:T(2,128)(2,1)S(1)} copy-done((bf16[1,2,1,1536]{3,1,2,0:T(2,128)(2,1)S(1)}, bf16[1,2,1,1536]{3,1,2,0:T(2,128)(2,1)}, u32[]{:S(2)}) %copy-start.3) | copy-done | bytes 6168
  4.7 0.0 copy-start.4
  4.7 0.7 %copy-done.4 = f32[192]{0:T(256)S(1)} copy-done((f32[192]{0:T(256)S(1)}, f32[192]{0:T(256)}, u32[]{:S(2)}) %copy-start.4) | copy-done | bytes 792
  5.4 59.6 %shard_map.76 = (bf16[12,1536]{1,0:T(8,128)(2,1)S(1)}, f32[27,72]{1,0:T(8,128)S(1)}, f32[1,192]{1,0:T(1,128)S(1)}) custom-call(bf16[12,1536]{1,0:T(8,128)(2,1)S(1)} %bitcast.9, bf16[2,1536]{1,0:T(2,128)(2,1)S(1)} %bitcast.11, f32[1,192]{1,0:T(1,128)S(1)} %bitcast.12, bf16[27,36864]{1,0:T(8,128)(2,1)S(1)} %copy-done, bf16[12,2,3072]{2,1,0:T(2,128)(2,1)S(1)} %bitcast.7), custom_call_target="tpu_custom_call" | custom-call | tf_op jit(solution)/shard_map/pallas_call | solution.py:350
  64.9 0.6 copy.8
  65.6 0.6 copy.11
  66.2 0.6 copy.12
Async XLA Ops:
  0.6 1.7 %copy-start = (bf16[27,36864]{1,0:T(8,128)(2,1)S(1)}, bf16[27,36864]{1,0:T(8,128)(2,1)}, u32[]{:S(2)}) copy-start(bf16[27,36864]{1,0:T(8,128)(2,1)} %w_ref.1) | copy-start | bytes 5971972
  2.3 0.9 %copy-start.1 = (bf16[1,12,2,3072]{3,2,1,0:T(2,128)(2,1)S(1)}, bf16[1,12,2,3072]{3,2,1,0:T(2,128)(2,1)}, u32[]{:S(2)}) copy-start(bf16[1,12,2,3072]{3,2,1,0:T(2,128)(2,1)} %param.9) | copy-start | bytes 442372
  3.2 0.8 %copy-start.2 = (bf16[1,12,1,1536]{3,1,2,0:T(8,128)(2,1)S(1)}, bf16[1,12,1,1536]{3,1,2,0:T(8,128)(2,1)}, u32[]{:S(2)}) copy-start(bf16[1,12,1,1536]{3,1,2,0:T(8,128)(2,1)} %param.5) | copy-start | bytes 110596
  4.0 0.7 %copy-start.3 = (bf16[1,2,1,1536]{3,1,2,0:T(2,128)(2,1)S(1)}, bf16[1,2,1,1536]{3,1,2,0:T(2,128)(2,1)}, u32[]{:S(2)}) copy-start(bf16[1,2,1,1536]{3,1,2,0:T(2,128)(2,1)} %param.6) | copy-start | bytes 18436
  4.7 0.7 %copy-start.4 = (f32[192]{0:T(256)S(1)}, f32[192]{0:T(256)}, u32[]{:S(2)}) copy-start(f32[192]{0:T(256)} %param.7) | copy-start | bytes 2308

commit v2 on v1

v2 whole, which is shorter than its diff:
```python
import functools

import jax
import jax.numpy as jnp
from jax import lax
from jax.experimental import pallas as pl
from jax.experimental.pallas import tpu as pltpu
from jax.sharding import PartitionSpec as P

CH = 192
T = 12
S = 8
TP = 16
ROWS = S * TP
HALF = 896
MESH = pl.DeviceIdType.MESH
F32 = jnp.float32
BF16 = jnp.bfloat16
NT = (((1,), (1,)), ((), ()))


def remote(src, dst, send, recv, device):
    return pltpu.make_async_remote_copy(
        src_ref=src, dst_ref=dst, send_sem=send, recv_sem=recv, device_id=device, device_id_type=MESH
    )


def kernel(
    x_hbm, car_hbm, gain_hbm, w_hbm, cot_hbm,
    gi_ref, gw_ref, gg_ref,
    x_ref, car_ref, gain_ref, cv, cf, fr, rb, hb, colh, wv, ws, wt, uf, ut, dk, p, r1, t2, q2, r2, vs, zb, r3,
    gh, gz, gc,
    in_sem, halo_s, halo_r, core_s, core_r, s1s, s1r, s2s, s2r, s3s, s3r, ghs, ghr, gzs, gzr, gcs, gcr,
):
    ha = lax.axis_index("ha")
    wa = lax.axis_index("wa")
    col = lax.axis_index("col")
    qy, qx = ha // 4, ha % 4
    up, down = (ha + 15) % 16, (ha + 1) % 16
    left, right = (wa + 15) % 16, (wa + 1) % 16
    other = 1 - col

    barrier = pltpu.get_barrier_semaphore()
    loads = [
        pltpu.make_async_copy(src, dst, in_sem.at[n])
        for n, (src, dst) in enumerate(
            ((cot_hbm, cv), (x_hbm, x_ref), (car_hbm, car_ref), (gain_hbm, gain_ref), (w_hbm, wv))
        )
    ]
    for load in loads:
        load.start()
    pl.semaphore_signal(barrier, inc=1, device_id=(ha, wa, other), device_id_type=MESH)
    for h in (up, down):
        for w in (left, right):
            pl.semaphore_signal(barrier, inc=1, device_id=(h, w, col), device_id_type=MESH)

    def greet(d, _):
        pl.semaphore_signal(barrier, inc=1, device_id=((ha + d) % 16, wa, col), device_id_type=MESH)
        pl.semaphore_signal(barrier, inc=1, device_id=(ha, (wa + d) % 16, col), device_id_type=MESH)
        return 0

    lax.fori_loop(1, 16, greet, 0)

    loads[0].wait()
    cf[...] = cv[...].astype(F32)
    pad4 = jnp.zeros((TP - T, 128), F32)
    for row in range(2):
        for lt in range(24):
            value = jnp.concatenate([cf[pl.ds(2 * lt + row, T, stride=48), :], pad4], axis=0)
            fr[row, lt] = value
            rb[row, lt] = value.astype(BF16)

    pl.semaphore_wait(barrier, 35)

    halos = []

    def halo(src, dst, device):
        n = len(halos)
        copy = remote(src, dst, halo_s.at[n], halo_r.at[n], device)
        copy.start()
        halos.append(copy)

    first_two, last_two = pl.ds(0, 2), pl.ds(22, 2)
    halo(rb.at[0], hb.at[1], (up, wa, col))
    halo(rb.at[1], hb.at[0], (down, wa, col))
    halo(rb.at[:, first_two], colh.at[1, pl.ds(1, 2)], (ha, left, col))
    halo(rb.at[:, last_two], colh.at[0, pl.ds(1, 2)], (ha, right, col))
    halo(rb.at[0, first_two], colh.at[1, 3], (up, left, col))
    halo(rb.at[0, last_two], colh.at[0, 3], (up, right, col))
    halo(rb.at[1, first_two], colh.at[1, 0], (down, left, col))
    halo(rb.at[1, last_two], colh.at[0, 0], (down, right, col))

    for load in loads[1:4]:
        load.wait()
    gain = gain_ref[...]
    pad = jnp.zeros((TP - T, CH), F32)
    x = jnp.concatenate(
        [piece for s in range(S) for piece in (x_ref[:, s * CH : (s + 1) * CH].astype(F32), pad)], axis=0
    )
    scale = lax.rsqrt(jnp.mean(x * x, axis=-1, keepdims=True) + 1e-06)
    normed = x * scale
    act = normed * gain
    sig = 1.0 / (1.0 + jnp.exp(-act))
    activated = (act * sig).astype(BF16).astype(F32).reshape(S, TP, CH)
    for s in range(S):
        uf[s, 0:2, :] = car_ref[:, s * CH : (s + 1) * CH].astype(F32)
        uf[s, 2 : 2 + TP, :] = activated[s]

    m = lax.broadcasted_iota(jnp.int32, (96, CH), 0)
    lane = lax.broadcasted_iota(jnp.int32, (96, CH), 1)
    first = (m >= 24).astype(jnp.int32) + (m >= 48).astype(jnp.int32) + (m >= 72).astype(jnp.int32)
    rest = m - 24 * first
    second = (rest >= 6).astype(jnp.int32) + (rest >= 12).astype(jnp.int32) + (rest >= 18).astype(jnp.int32)
    swapped = 24 * second + 6 * first + (rest - 6 * second)
    u = jnp.concatenate([uf[:, a : a + TP, :].reshape(ROWS, CH).astype(BF16) for a in range(3)], axis=0)
    for k, half in ((2, other), (0, col)):
        for hf, channel in enumerate((m, swapped)):
            sel = (lane == channel + 96 * half).astype(F32).astype(BF16)
            moved = lax.dot_general(sel, u, NT, preferred_element_type=F32).astype(BF16)
            for a in range(3):
                ut[k, hf, a] = moved[:, a * ROWS : (a + 1) * ROWS]
        if k == 2:
            u_copy = remote(ut.at[2], ut.at[1], core_s.at[0], core_r.at[0], (ha, wa, other))
            u_copy.start()

    for copy in halos:
        copy.wait_recv()
    top = (ha > 0).astype(F32)
    bottom = (ha < 15).astype(F32)
    at_left = (wa > 0).astype(F32)
    at_right = (wa < 15).astype(F32)
    low_lanes = lax.broadcasted_iota(jnp.int32, (TP, 128), 1) < 64

    def turn(tile):
        return pltpu.roll(tile, 64, axis=1)

    def row_sum(b, load):
        one, two = load(b)
        if b == 0:
            two = two * bottom
        if b == 2:
            one = one * top
        return one + two

    def own_rows(lt):
        def load(b):
            if b == 0:
                return fr[1, lt], hb[1, lt].astype(F32)
            if b == 1:
                return fr[0, lt], fr[1, lt]
            return hb[0, lt].astype(F32), fr[0, lt]

        return load

    def side_rows(side, k):
        def load(b):
            return colh[side, 2 - b, k].astype(F32), colh[side, 3 - b, k].astype(F32)

        return load

    columns = {}

    def column(b, j):
        if (b, j) not in columns:
            if j == -1:
                pair = [row_sum(b, side_rows(0, k)) * at_left for k in range(2)]
            elif j == 2 * S:
                pair = [row_sum(b, side_rows(1, k)) * at_right for k in range(2)]
            else:
                pair = [row_sum(b, own_rows(3 * (j // 2) + j % 2 + k)) for k in range(2)]
            turned = [turn(pair[0]), turn(pair[1])]
            if j % 2 == 0:
                moved = [turned[0], jnp.where(low_lanes, turned[0], turned[1])]
            else:
                moved = [jnp.where(low_lanes, turned[0], turned[1]), turned[1]]
            columns[b, j] = (pair, moved)
        return columns[b, j]

    def cells(be, s, k):
        b, e = be // 3, be % 3
        j = 2 * s + 1 - e
        total = None
        for c in (j, j + 1):
            natural, moved = column(b, c)
            tile = natural[k] if c % 2 == be % 2 else moved[k]
            total = tile if total is None else total + tile
        return total

    d_copies = []
    for hf in range(2):
        for s in range(S):
            for n in range(7 * hf, 7 * hf + 7):
                be, k = 2 * (n // 3), n % 3
                if k == 0:
                    tile = cells(be, s, 0)
                elif k == 1:
                    tile = jnp.where(low_lanes, cells(be, s, 1), cells(be + 1, s, 0) if be < 8 else 0.0)
                else:
                    tile = cells(be + 1, s, 1)
                high = tile.astype(BF16)
                low = (tile - high.astype(F32)).astype(BF16)
                dk[s * TP : (s + 1) * TP, n * 128 : (n + 1) * 128] = high
                dk[ROWS + s * TP : ROWS + (s + 1) * TP, n * 128 : (n + 1) * 128] = low
        lanes = pl.ds(hf * HALF, HALF)
        copy = remote(
            dk.at[pl.ds(0, 2 * ROWS), lanes], dk.at[pl.ds(2 * ROWS, 2 * ROWS), lanes],
            core_s.at[1 + hf], core_r.at[1 + hf], (ha, wa, other),
        )
        copy.start()
        d_copies.append(copy)

    loads[4].wait()

    def widen(n, _):
        lanes = pl.ds(pl.multiple_of(n * 128, 128), 128)
        for t8 in range(4):
            count = 8 if t8 < 3 else 3
            at = pl.multiple_of((t8 * 288 + n) * 8, 8)
            ws[pl.ds(at, count), :] = wv[t8 * 8 : t8 * 8 + count, lanes].astype(F32)
        return 0

    lax.fori_loop(0, 288, widen, 0, unroll=8)
    low_wide = lax.broadcasted_iota(jnp.int32, (96, 128), 1) < 64
    for a in range(3):
        for parity in range(2):
            at = a * 256 + parity * 128
            wt[at + 96 : at + 128, :] = jnp.zeros((32, 2 * HALF), BF16)
        even = slice(a * 256, a * 256 + 96)
        odd = slice(a * 256 + 128, a * 256 + 224)
        for k in range(5):

            def tap(be, j):
                t8, tr = (9 * a + be) // 8, (9 * a + be) % 8
                return ws[pl.ds((t8 * 288 + j) * 8 + tr, 96, stride=24), :]

            a0, a1, a2 = (tap(2 * k, j) for j in range(3))
            t1, t2w = turn(a1), turn(a2)
            at = k * 384
            wt[even, at : at + 128] = a0.astype(BF16)
            wt[odd, at : at + 128] = jnp.where(low_wide, t1, t2w).astype(BF16)
            if k < 4:
                b0, b1, b2 = (tap(2 * k + 1, j) for j in range(3))
                s0, s1 = turn(b0), turn(b1)
                wt[even, at + 128 : at + 256] = jnp.where(low_wide, a1, s0).astype(BF16)
                wt[even, at + 256 : at + 384] = jnp.where(low_wide, s0, s1).astype(BF16)
                wt[odd, at + 128 : at + 256] = jnp.where(low_wide, t2w, b1).astype(BF16)
                wt[odd, at + 256 : at + 384] = b2.astype(BF16)
            else:
                wt[even, at + 128 : at + 256] = jnp.where(low_wide, a1, 0.0).astype(BF16)
                wt[odd, at + 128 : at + 256] = jnp.where(low_wide, t2w, 0.0).astype(BF16)

    def ring(hf, d):
        if hf == 0:
            return ((qy + d) % 4) * 4 + qx
        return qy * 4 + (qx + d) % 4

    mine = (qy, qx)
    u_copy.wait_recv()
    ones = {}
    for hf in range(2):
        d_copies[hf].wait_recv()
        own, his = (ut[k, hf].reshape(288, ROWS) for k in range(2))
        lhs = jnp.concatenate([own, own, his, his], axis=1)
        part = jnp.dot(lhs, dk[:, hf * HALF : (hf + 1) * HALF], preferred_element_type=F32)
        p[hf] = part.reshape(3, 4, 24, HALF)
        for a in range(3):
            for d in range(1, 4):
                copy = remote(
                    p.at[hf, a, (mine[hf] + d) % 4], r1.at[a, hf, d - 1], s1s.at[a, hf, d - 1], s1r.at[a, hf, d - 1],
                    (ring(hf, d), wa, col),
                )
                copy.start()
                ones[a, hf, d] = copy

    g = lax.dot_general(dk[0 : 2 * ROWS, :], wt[...], NT, preferred_element_type=F32)
    g = g[0:ROWS] + g[ROWS : 2 * ROWS]
    g = g[:, 512:768] + pltpu.roll(g[:, 256:512], ROWS - 1, axis=0) + pltpu.roll(g[:, 0:256], ROWS - 2, axis=0)
    k = lax.broadcasted_iota(jnp.int32, (256, CH), 0)
    chan = lax.broadcasted_iota(jnp.int32, (256, CH), 1)
    spread = (chan == jnp.where(k < 128, 2 * k, 2 * (k - 128) + 1)).astype(F32).astype(BF16)
    high = g.astype(BF16)
    low = (g - high.astype(F32)).astype(BF16)
    coarse = jnp.dot(jnp.concatenate([high, low], axis=0), spread, preferred_element_type=F32)
    coarse = coarse[0:ROWS] + coarse[ROWS : 2 * ROWS]
    grad_act = coarse * (sig * (1.0 + act * (1.0 - sig)))
    gain_term = jnp.sum(grad_act * normed, axis=0, keepdims=True)
    gh[ha] = jnp.concatenate([gain_term, jnp.zeros((1, 64), F32)], axis=1)

    def gh_send(d, _):
        remote(gh.at[ha], gh.at[ha], ghs.at[d - 1], ghr.at[d - 1], ((ha + d) % 16, wa, col)).start()
        return 0

    lax.fori_loop(1, 16, gh_send, 0)
    grad_normed = grad_act * gain
    grad_in = scale * (grad_normed - normed * jnp.mean(grad_normed * normed, axis=-1, keepdims=True))
    for s in range(S):
        gi_ref[:, s * CH : (s + 1) * CH] = grad_in[s * TP : s * TP + T].astype(BF16)

    twos = {}
    for a in range(3):
        for hf in range(2):
            for d in range(1, 4):
                ones[a, hf, d].wait_recv()
            total = p[hf, a, mine[hf]] + r1[a, hf, 0] + r1[a, hf, 1] + r1[a, hf, 2]
            t2[0:24, :] = total
            t2[24:32, :] = jnp.zeros((8, HALF), F32)
            for k in range(4):
                q2[a, hf, k] = t2[6 * k : 6 * k + 8, :]
            for d in range(1, 4):
                copy = remote(
                    q2.at[a, hf, (mine[1 - hf] + d) % 4], r2.at[a, hf, d - 1], s2s.at[a, hf, d - 1],
                    s2r.at[a, hf, d - 1], (ring(1 - hf, d), wa, col),
                )
                copy.start()
                twos[a, hf, d] = copy

    def gh_wait(d, _):
        src = (ha + 16 - d) % 16
        remote(gh.at[ha], gh.at[src], ghs.at[d - 1], ghr.at[d - 1], (src, wa, col)).wait_recv()
        return 0

    lax.fori_loop(1, 16, gh_wait, 0)
    gz[wa] = jnp.sum(gh[...], axis=0)

    def gz_send(d, _):
        remote(gz.at[wa], gz.at[wa], gzs.at[d - 1], gzr.at[d - 1], (ha, (wa + d) % 16, col)).start()
        return 0

    lax.fori_loop(1, 16, gz_send, 0)

    for a in range(3):
        for hf in range(2):
            for d in range(1, 4):
                twos[a, hf, d].wait_recv()
            total = q2[a, hf, mine[1 - hf]] + r2[a, hf, 0] + r2[a, hf, 1] + r2[a, hf, 2]
            for k in range(7):
                at = (7 * hf + k) * 8
                vs[a, at : at + 8, :] = total[:, k * 128 : (k + 1) * 128]
        vs[a, 112:192, :] = jnp.zeros((80, 128), F32)
        y = []
        for i in range(6):
            tiles = jnp.concatenate([vs[a, pl.ds(j * 8 + i, 8, stride=24), :] for j in range(3)], axis=1)
            y.append((tiles[:, 0:CH], tiles[:, CH : 2 * CH]))
        for w in range(16):
            i0, o0 = (72 * w) // CH, (72 * w) % CH
            n0 = min(72, CH - o0)
            pieces = []
            for parity in range(2):
                pieces.append(y[i0][parity][:, o0 : o0 + n0])
                if n0 < 72:
                    pieces.append(y[i0 + 1][parity][:, 0 : 72 - n0])
            tile = jnp.concatenate(pieces, axis=1)
            zb[a, w] = tile[:, 0:128]
            spare = jnp.concatenate([tile[k : k + 1, 128:144] for k in range(4)], axis=1)
            zb[a, w, 5:6, 0:64] = spare

        def z_send(d, _):
            remote(
                zb.at[a, (wa + d) % 16], r3.at[a, d - 1], s3s.at[a, d - 1], s3r.at[a, d - 1],
                (ha, (wa + d) % 16, col),
            ).start()
            return 0

        lax.fori_loop(1, 16, z_send, 0)

    def gz_wait(d, _):
        src = (wa + 16 - d) % 16
        remote(gz.at[wa], gz.at[src], gzs.at[d - 1], gzr.at[d - 1], (ha, src, col)).wait_recv()
        return 0

    lax.fori_loop(1, 16, gz_wait, 0)
    gc[0] = jnp.sum(gz[...], axis=0)
    gc_copy = remote(gc.at[0], gc.at[1], gcs, gcr, (ha, wa, other))
    gc_copy.start()

    for a in range(3):

        def z_wait(d, _):
            remote(
                zb.at[a, (wa + d) % 16], r3.at[a, d - 1], s3s.at[a, d - 1], s3r.at[a, d - 1],
                (ha, (wa + d) % 16, col),
            ).wait()
            return 0

        lax.fori_loop(1, 16, z_wait, 0)
        total = zb[a, wa] + jnp.sum(r3[a], axis=0)
        for be in range(9):
            k = be // 2
            if be % 2 == 0:
                row = total[k : k + 1, 0:72]
            else:
                row = jnp.concatenate([total[k : k + 1, 72:128], total[5:6, 16 * k : 16 * k + 16]], axis=1)
            gw_ref[9 * a + be : 9 * a + be + 1, :] = row

    gc_copy.wait()
    gg_ref[...] = (gc[0] + gc[1])[:, 0:CH]

    for copy in halos + d_copies + [u_copy] + list(ones.values()) + list(twos.values()):
        copy.wait_send()

    def g_done(d, _):
        remote(gh.at[ha], gh.at[ha], ghs.at[d - 1], ghr.at[d - 1], ((ha + d) % 16, wa, col)).wait_send()
        remote(gz.at[wa], gz.at[wa], gzs.at[d - 1], gzr.at[d - 1], (ha, (wa + d) % 16, col)).wait_send()
        return 0

    lax.fori_loop(1, 16, g_done, 0)


def on_device(inputs, carried, gain, weight, cotangent):
    vmem = pl.BlockSpec(memory_space=pltpu.VMEM)
    hbm = pl.BlockSpec(memory_space=pl.ANY)
    dma = pltpu.SemaphoreType.DMA
    gi, gw, gg = pl.pallas_call(
        kernel,
        out_shape=(
            jax.ShapeDtypeStruct((T, S * CH), BF16),
            jax.ShapeDtypeStruct((27, 72), F32),
            jax.ShapeDtypeStruct((1, CH), F32),
        ),
        in_specs=[hbm] * 5,
        out_specs=(vmem, vmem, vmem),
        scratch_shapes=[
            pltpu.VMEM((T, S * CH), BF16),
            pltpu.VMEM((2, S * CH), BF16),
            pltpu.VMEM((1, CH), F32),
            pltpu.VMEM((576, 128), BF16),
            pltpu.VMEM((576, 128), F32),
            pltpu.VMEM((2, 24, TP, 128), F32),
            pltpu.VMEM((2, 24, TP, 128), BF16),
            pltpu.VMEM((2, 24, TP, 128), BF16),
            pltpu.VMEM((2, 4, 2, TP, 128), BF16),
            pltpu.VMEM((27, CH * CH), BF16),
            pltpu.VMEM((4 * 288 * 8, 128), F32),
            pltpu.VMEM((768, 2 * HALF), BF16),
            pltpu.VMEM((S, 24, CH), F32),
            pltpu.VMEM((3, 2, 3, 96, ROWS), BF16),
            pltpu.VMEM((4 * ROWS, 2 * HALF), BF16),
            pltpu.VMEM((2, 3, 4, 24, HALF), F32),
            pltpu.VMEM((3, 2, 3, 24, HALF), F32),
            pltpu.VMEM((32, HALF), F32),
            pltpu.VMEM((3, 2, 4, 8, HALF), F32),
            pltpu.VMEM((3, 2, 3, 8, HALF), F32),
            pltpu.VMEM((3, 192, 128), F32),
            pltpu.VMEM((3, 16, 8, 128), F32),
            pltpu.VMEM((3, 15, 8, 128), F32),
            pltpu.VMEM((16, 1, 256), F32),
            pltpu.VMEM((16, 1, 256), F32),
            pltpu.VMEM((2, 1, 256), F32),
            dma((5,)), dma((8,)), dma((8,)), dma((3,)), dma((3,)),
            dma((3, 2, 3)), dma((3, 2, 3)), dma((3, 2, 3)), dma((3, 2, 3)),
            dma((3, 15)), dma((3, 15)), dma((15,)), dma((15,)), dma((15,)), dma((15,)), dma(()), dma(()),
        ],
        compiler_params=pltpu.CompilerParams(
            collective_id=0, has_side_effects=True, vmem_limit_bytes=60 * 1024 * 1024
        ),
    )(
        inputs.reshape(T, S * CH),
        carried.reshape(2, S * CH),
        gain.reshape(1, CH),
        weight,
        cotangent.reshape(T, 2, 24, 128).transpose(0, 2, 1, 3).reshape(576, 128),
    )
    return gi.reshape(inputs.shape), gw.reshape(1, 27, 72), gg.reshape(CH)


def solution(mesh):
    placed = (
        P("col", None, "ha", "wa"),
        P("col", None, "ha", "wa"),
        P(),
        P(),
        P("col", None, "ha", "wa"),
    )
    return jax.shard_map(
        on_device,
        mesh=mesh,
        in_specs=placed,
        out_specs=(P("col", None, "ha", "wa"), P("col", None, ("ha", "wa")), P()),
        check_vma=False,
    )
```

time: 67 us -> 61.3 us (0.915)
  the two profiles are of different devices: /device:TPU:1 before, /device:TPU:4 now
where the time goes in v2:
time: 61.3 us; the launch traced here: 61.1 us
  Pallas kernels  56.5 us (92%)
  local copies, waits for them, and re-layouts  3.95 us (6%)
  between operations  0.64 us (1%)
    pallas_call x1, Pallas kernels, on_device(): pl.pallas_call(kernel, out_shape=(jax.ShapeDtypeStruct((T, S * CH), BF16)...  56.5 us
    unnamed x3, local copies, waits for them, and re-layouts  3.95 us

profile of v2, /device:TPU:4, one launch (start us, length us, event | category | flops | bytes accessed | tf_op | source)
XLA Modules:
  0.0 61.1 jit_solution(14537922051941876691)
XLA Ops:
  0.6 56.5 %shard_map.76 = (bf16[12,1536]{1,0:T(8,128)(2,1)}, f32[27,72]{1,0:T(8,128)}, f32[1,192]{1,0:T(1,128)}) custom-call(bf16[12,1536]{1,0:T(8,128)(2,1)} %bitcast.13, bf16[2,1536]{1,0:T(2,128)(2,1)} %bitcast.15, f32[1,192]{1,0:T(1,128)} %bitcast.16, bf16[27,36864]{1,0:T(8,128)(2,1)} %w_hbm.1, bf16[576,128]{1,0:T(8,128)(2,1)} %bitcast.11), custom_call_target="tpu_custom_call" | custom-call | tf_op jit(solution)/shard_map/pallas_call | solution.py:413
  57.1 1.3 %copy.9 = f32[1,27,72]{2,0,1:T(1,128)} copy(f32[1,27,72]{2,1,0:T(8,128)} %bitcast.14) | data formatting | bytes 15552
  58.5 1.4 %copy.12 = bf16[1,12,1,1536]{3,1,2,0:T(8,128)(2,1)} copy(bf16[1,12,1,1536]{3,1,2,0:T(8,128)(2,1)} %bitcast.12) | data formatting | bytes 73728
  59.9 1.2 %copy.13 = f32[192]{0:T(256)} copy(f32[192]{0:T(256)} %bitcast.17) | data formatting | bytes 1536

commit v3 on v2

--- a/solution.py
+++ b/solution.py
@@ -27,10 +27,10 @@
 
 def kernel(
     x_hbm, car_hbm, gain_hbm, w_hbm, cot_hbm,
-    gi_ref, gw_ref, gg_ref,
-    x_ref, car_ref, gain_ref, cv, cf, fr, rb, hb, colh, wv, ws, wt, uf, ut, dk, p, r1, t2, q2, r2, vs, zb, r3,
+    gi_hbm, gw_hbm, gg_hbm,
+    gi_ref, gw_ref, gg_ref, x_ref, car_ref, gain_ref, cv, cf, fr, rb, hb, colh, wv, ws, wt, uf, ut, dk, p, r0, r1, f0, t2, q2, r2, vs, zb, r3,
     gh, gz, gc,
-    in_sem, halo_s, halo_r, core_s, core_r, s1s, s1r, s2s, s2r, s3s, s3r, ghs, ghr, gzs, gzr, gcs, gcr,
+    in_sem, out_sem, halo_s, halo_r, core_s, core_r, s1s, s1r, s2s, s2r, s3s, s3r, ghs, ghr, gzs, gzr, gcs, gcr,
 ):
     ha = lax.axis_index("ha")
     wa = lax.axis_index("wa")
@@ -60,6 +60,9 @@
         return 0
 
     lax.fori_loop(1, 16, greet, 0)
+
+    vs[:, 112:192, :] = jnp.zeros((3, 80, 128), F32)
+    t2[24:32, :] = jnp.zeros((8, HALF), F32)
 
     loads[0].wait()
     cf[...] = cv[...].astype(F32)
@@ -257,22 +260,45 @@
     mine = (qy, qx)
     u_copy.wait_recv()
     ones = {}
+
+    def first_send(key, src, dst, hf, d):
+        a = key[0]
+        copy = remote(src, dst, s1s.at[a, hf, key[2]], s1r.at[a, hf, key[2]], (ring(hf, d), wa, col))
+        copy.start()
+        ones[key] = copy
+
+    def cut(a):
+        c = 512 if a % 2 == 0 else 384
+        return pl.ds(0, c), pl.ds(c, HALF - c)
+
     for hf in range(2):
         d_copies[hf].wait_recv()
         own, his = (ut[k, hf].reshape(288, ROWS) for k in range(2))
         lhs = jnp.concatenate([own, own, his, his], axis=1)
         part = jnp.dot(lhs, dk[:, hf * HALF : (hf + 1) * HALF], preferred_element_type=F32)
         p[hf] = part.reshape(3, 4, 24, HALF)
+        q = mine[hf]
         for a in range(3):
-            for d in range(1, 4):
-                copy = remote(
-                    p.at[hf, a, (mine[hf] + d) % 4], r1.at[a, hf, d - 1], s1s.at[a, hf, d - 1], s1r.at[a, hf, d - 1],
-                    (ring(hf, d), wa, col),
-                )
-                copy.start()
-                ones[a, hf, d] = copy
+            one, two = cut(a)
+            far, near, back = (q + 2) % 4, (q + 1) % 4, (q + 3) % 4
+            first_send((a, hf, 0), p.at[hf, a, far, :, one], r0.at[a, hf, :, one], hf, 1)
+            first_send((a, hf, 1), p.at[hf, a, far, :, two], r0.at[a, hf, :, two], hf, 3)
+            first_send((a, hf, 2), p.at[hf, a, near, :, two], r1.at[a, hf, 0, :, two], hf, 1)
+            first_send((a, hf, 3), p.at[hf, a, back, :, one], r1.at[a, hf, 1, :, one], hf, 3)
+
+    def pass_on(a):
+        one, two = cut(a)
+        for hf in range(2):
+            near, back = (mine[hf] + 1) % 4, (mine[hf] + 3) % 4
+            ones[a, hf, 0].wait_recv()
+            f0[a, hf, :, one] = p[hf, a, near, :, one] + r0[a, hf, :, one]
+            first_send((a, hf, 4), f0.at[a, hf, :, one], r1.at[a, hf, 0, :, one], hf, 1)
+            ones[a, hf, 1].wait_recv()
+            f0[a, hf, :, two] = p[hf, a, back, :, two] + r0[a, hf, :, two]
+            first_send((a, hf, 5), f0.at[a, hf, :, two], r1.at[a, hf, 1, :, two], hf, 3)
 
     g = lax.dot_general(dk[0 : 2 * ROWS, :], wt[...], NT, preferred_element_type=F32)
+    pass_on(0)
     g = g[0:ROWS] + g[ROWS : 2 * ROWS]
     g = g[:, 512:768] + pltpu.roll(g[:, 256:512], ROWS - 1, axis=0) + pltpu.roll(g[:, 0:256], ROWS - 2, axis=0)
     k = lax.broadcasted_iota(jnp.int32, (256, CH), 0)
@@ -282,6 +308,7 @@
     low = (g - high.astype(F32)).astype(BF16)
     coarse = jnp.dot(jnp.concatenate([high, low], axis=0), spread, preferred_element_type=F32)
     coarse = coarse[0:ROWS] + coarse[ROWS : 2 * ROWS]
+    pass_on(1)
     grad_act = coarse * (sig * (1.0 + act * (1.0 - sig)))
     gain_term = jnp.sum(grad_act * normed, axis=0, keepdims=True)
     gh[ha] = jnp.concatenate([gain_term, jnp.zeros((1, 64), F32)], axis=1)
@@ -291,19 +318,21 @@
         return 0
 
     lax.fori_loop(1, 16, gh_send, 0)
+    pass_on(2)
     grad_normed = grad_act * gain
     grad_in = scale * (grad_normed - normed * jnp.mean(grad_normed * normed, axis=-1, keepdims=True))
     for s in range(S):
         gi_ref[:, s * CH : (s + 1) * CH] = grad_in[s * TP : s * TP + T].astype(BF16)
+    gi_out = pltpu.make_async_copy(gi_ref, gi_hbm, out_sem.at[0])
+    gi_out.start()
 
     twos = {}
-    for a in range(3):
+
+    def second(a):
         for hf in range(2):
-            for d in range(1, 4):
-                ones[a, hf, d].wait_recv()
-            total = p[hf, a, mine[hf]] + r1[a, hf, 0] + r1[a, hf, 1] + r1[a, hf, 2]
-            t2[0:24, :] = total
-            t2[24:32, :] = jnp.zeros((8, HALF), F32)
+            for n in range(2, 6):
+                ones[a, hf, n].wait_recv()
+            t2[0:24, :] = p[hf, a, mine[hf]] + r1[a, hf, 0] + r1[a, hf, 1]
             for k in range(4):
                 q2[a, hf, k] = t2[6 * k : 6 * k + 8, :]
             for d in range(1, 4):
@@ -314,21 +343,7 @@
                 copy.start()
                 twos[a, hf, d] = copy
 
-    def gh_wait(d, _):
-        src = (ha + 16 - d) % 16
-        remote(gh.at[ha], gh.at[src], ghs.at[d - 1], ghr.at[d - 1], (src, wa, col)).wait_recv()
-        return 0
-
-    lax.fori_loop(1, 16, gh_wait, 0)
-    gz[wa] = jnp.sum(gh[...], axis=0)
-
-    def gz_send(d, _):
-        remote(gz.at[wa], gz.at[wa], gzs.at[d - 1], gzr.at[d - 1], (ha, (wa + d) % 16, col)).start()
-        return 0
-
-    lax.fori_loop(1, 16, gz_send, 0)
-
-    for a in range(3):
+    def third(a):
         for hf in range(2):
             for d in range(1, 4):
                 twos[a, hf, d].wait_recv()
@@ -336,7 +351,6 @@
             for k in range(7):
                 at = (7 * hf + k) * 8
                 vs[a, at : at + 8, :] = total[:, k * 128 : (k + 1) * 128]
-        vs[a, 112:192, :] = jnp.zeros((80, 128), F32)
         y = []
         for i in range(6):
             tiles = jnp.concatenate([vs[a, pl.ds(j * 8 + i, 8, stride=24), :] for j in range(3)], axis=1)
@@ -363,18 +377,7 @@
 
         lax.fori_loop(1, 16, z_send, 0)
 
-    def gz_wait(d, _):
-        src = (wa + 16 - d) % 16
-        remote(gz.at[wa], gz.at[src], gzs.at[d - 1], gzr.at[d - 1], (ha, src, col)).wait_recv()
-        return 0
-
-    lax.fori_loop(1, 16, gz_wait, 0)
-    gc[0] = jnp.sum(gz[...], axis=0)
-    gc_copy = remote(gc.at[0], gc.at[1], gcs, gcr, (ha, wa, other))
-    gc_copy.start()
-
-    for a in range(3):
-
+    def finish(a):
         def z_wait(d, _):
             remote(
                 zb.at[a, (wa + d) % 16], r3.at[a, d - 1], s3s.at[a, d - 1], s3r.at[a, d - 1],
@@ -390,10 +393,44 @@
                 row = total[k : k + 1, 0:72]
             else:
                 row = jnp.concatenate([total[k : k + 1, 72:128], total[5:6, 16 * k : 16 * k + 16]], axis=1)
-            gw_ref[9 * a + be : 9 * a + be + 1, :] = row
-
+            gw_ref[9 * a + be] = row
+
+    def gh_wait(d, _):
+        src = (ha + 16 - d) % 16
+        remote(gh.at[ha], gh.at[src], ghs.at[d - 1], ghr.at[d - 1], (src, wa, col)).wait_recv()
+        return 0
+
+    def gz_send(d, _):
+        remote(gz.at[wa], gz.at[wa], gzs.at[d - 1], gzr.at[d - 1], (ha, (wa + d) % 16, col)).start()
+        return 0
+
+    def gz_wait(d, _):
+        src = (wa + 16 - d) % 16
+        remote(gz.at[wa], gz.at[src], gzs.at[d - 1], gzr.at[d - 1], (ha, src, col)).wait_recv()
+        return 0
+
+    second(0)
+    second(1)
+    lax.fori_loop(1, 16, gh_wait, 0)
+    gz[wa] = jnp.sum(gh[...], axis=0)
+    lax.fori_loop(1, 16, gz_send, 0)
+    third(0)
+    second(2)
+    third(1)
+    lax.fori_loop(1, 16, gz_wait, 0)
+    gc[0] = jnp.sum(gz[...], axis=0)
+    gc_copy = remote(gc.at[0], gc.at[1], gcs, gcr, (ha, wa, other))
+    gc_copy.start()
+    third(2)
+    finish(0)
     gc_copy.wait()
     gg_ref[...] = (gc[0] + gc[1])[:, 0:CH]
+    gg_out = pltpu.make_async_copy(gg_ref, gg_hbm, out_sem.at[1])
+    gg_out.start()
+    finish(1)
+    finish(2)
+    gw_out = pltpu.make_async_copy(gw_ref, gw_hbm, out_sem.at[2])
+    gw_out.start()
 
     for copy in halos + d_copies + [u_copy] + list(ones.values()) + list(twos.values()):
         copy.wait_send()
@@ -404,22 +441,38 @@
         return 0
 
     lax.fori_loop(1, 16, g_done, 0)
+    for copy in (gi_out, gg_out, gw_out):
+        copy.wait()
+
+
+def hand_on(gi_from, gw_from, gg_from, gi_to, gw_to, gg_to, sem):
+    copies = [
+        pltpu.make_async_copy(src, dst, sem.at[n])
+        for n, (src, dst) in enumerate(((gi_from, gi_to), (gw_from, gw_to), (gg_from, gg_to)))
+    ]
+    for copy in copies:
+        copy.start()
+    for copy in copies:
+        copy.wait()
 
 
 def on_device(inputs, carried, gain, weight, cotangent):
-    vmem = pl.BlockSpec(memory_space=pltpu.VMEM)
     hbm = pl.BlockSpec(memory_space=pl.ANY)
     dma = pltpu.SemaphoreType.DMA
-    gi, gw, gg = pl.pallas_call(
+    outs = (
+        jax.ShapeDtypeStruct((T, S * CH), BF16),
+        jax.ShapeDtypeStruct((27, 1, 72), F32),
+        jax.ShapeDtypeStruct((1, CH), F32),
+    )
+    results = pl.pallas_call(
         kernel,
-        out_shape=(
-            jax.ShapeDtypeStruct((T, S * CH), BF16),
-            jax.ShapeDtypeStruct((27, 72), F32),
-            jax.ShapeDtypeStruct((1, CH), F32),
-        ),
+        out_shape=outs,
         in_specs=[hbm] * 5,
-        out_specs=(vmem, vmem, vmem),
+        out_specs=(hbm, hbm, hbm),
         scratch_shapes=[
+            pltpu.VMEM((T, S * CH), BF16),
+            pltpu.VMEM((27, 1, 72), F32),
+            pltpu.VMEM((1, CH), F32),
             pltpu.VMEM((T, S * CH), BF16),
             pltpu.VMEM((2, S * CH), BF16),
             pltpu.VMEM((1, CH), F32),
@@ -436,7 +489,9 @@
             pltpu.VMEM((3, 2, 3, 96, ROWS), BF16),
             pltpu.VMEM((4 * ROWS, 2 * HALF), BF16),
             pltpu.VMEM((2, 3, 4, 24, HALF), F32),
-            pltpu.VMEM((3, 2, 3, 24, HALF), F32),
+            pltpu.VMEM((3, 2, 24, HALF), F32),
+            pltpu.VMEM((3, 2, 2, 24, HALF), F32),
+            pltpu.VMEM((3, 2, 24, HALF), F32),
             pltpu.VMEM((32, HALF), F32),
             pltpu.VMEM((3, 2, 4, 8, HALF), F32),
             pltpu.VMEM((3, 2, 3, 8, HALF), F32),
@@ -446,12 +501,12 @@
             pltpu.VMEM((16, 1, 256), F32),
             pltpu.VMEM((16, 1, 256), F32),
             pltpu.VMEM((2, 1, 256), F32),
-            dma((5,)), dma((8,)), dma((8,)), dma((3,)), dma((3,)),
-            dma((3, 2, 3)), dma((3, 2, 3)), dma((3, 2, 3)), dma((3, 2, 3)),
+            dma((5,)), dma((3,)), dma((8,)), dma((8,)), dma((3,)), dma((3,)),
+            dma((3, 2, 6)), dma((3, 2, 6)), dma((3, 2, 3)), dma((3, 2, 3)),
             dma((3, 15)), dma((3, 15)), dma((15,)), dma((15,)), dma((15,)), dma((15,)), dma(()), dma(()),
         ],
         compiler_params=pltpu.CompilerParams(
-            collective_id=0, has_side_effects=True, vmem_limit_bytes=60 * 1024 * 1024
+            collective_id=0, has_side_effects=True, vmem_limit_bytes=62 * 1024 * 1024
         ),
     )(
         inputs.reshape(T, S * CH),
@@ -460,6 +515,10 @@
         weight,
         cotangent.reshape(T, 2, 24, 128).transpose(0, 2, 1, 3).reshape(576, 128),
     )
+    gi, gw, gg = pl.pallas_call(
+        hand_on, out_shape=outs, in_specs=[hbm] * 3, out_specs=(hbm, hbm, hbm), scratch_shapes=[dma((3,))],
+        compiler_params=pltpu.CompilerParams(vmem_limit_bytes=62 * 1024 * 1024),
+    )(*results)
     return gi.reshape(inputs.shape), gw.reshape(1, 27, 72), gg.reshape(CH)
 
 

time: 61.3 us -> 58.7 us (0.958)
  the two profiles are of different devices: /device:TPU:4 before, /device:TPU:6 now
where the time goes in v3:
time: 58.7 us; the launch traced here: 58.6 us
  Pallas kernels  57.9 us (99%)
  between operations  0.64 us (1%)
    pallas_call x1, Pallas kernels, on_device(): pl.pallas_call(kernel, out_shape=outs, in_specs=[hbm] * 5, out_specs=(hbm...  54.9 us
    pallas_call x1, Pallas kernels, on_device(): pl.pallas_call(hand_on, out_shape=outs, in_specs=[hbm] * 3, out_specs=(hb...  3.07 us

profile of v3, /device:TPU:6, one launch (start us, length us, event | category | flops | bytes accessed | tf_op | source)
XLA Modules:
  0.0 58.6 jit_solution(11583867906702629523)
XLA Ops:
  0.6 54.9 %shard_map.76 = (bf16[12,1536]{1,0:T(8,128)(2,1)}, f32[27,1,72]{2,1,0:T(1,128)}, f32[1,192]{1,0:T(1,128)}) custom-call(bf16[12,1536]{1,0:T(8,128)(2,1)} %bitcast.12, bf16[2,1536]{1,0:T(2,128)(2,1)} %bitcast.13, f32[1,192]{1,0:T(1,128)} %bitcast.14, bf16[27,36864]{1,0:T(8,128)(2,1)} %w_hbm.1, bf16[576,128]{1,0:T(8,128)(2,1)} %bitcast.11), custom_call_target="tpu_custom_call" | custom-call | tf_op jit(solution)/shard_map/pallas_call | solution.py:467
  55.5 3.1 %shard_map.77 = (bf16[12,1536]{1,0:T(8,128)(2,1)}, f32[27,1,72]{2,1,0:T(1,128)}, f32[1,192]{1,0:T(1,128)}) custom-call(bf16[12,1536]{1,0:T(8,128)(2,1)} %get-tuple-element.9.gi_from, f32[27,1,72]{2,1,0:T(1,128)} %get-tuple-element.10.gw_from, f32[1,192]{1,0:T(1,128)} %get-tuple-element.11.gg_from), custom_call_target="tpu_custom_call" | custom-call | tf_op jit(solution)/shard_map/pallas_call | solution.py:518

commit v4 on v3

--- a/solution.py
+++ b/solution.py
@@ -271,20 +271,26 @@
         c = 512 if a % 2 == 0 else 384
         return pl.ds(0, c), pl.ds(c, HALF - c)
 
+    def first(a, hf):
+        q = mine[hf]
+        one, two = cut(a)
+        far, near, back = (q + 2) % 4, (q + 1) % 4, (q + 3) % 4
+        first_send((a, hf, 0), p.at[hf, a, far, :, one], r0.at[a, hf, :, one], hf, 1)
+        first_send((a, hf, 1), p.at[hf, a, far, :, two], r0.at[a, hf, :, two], hf, 3)
+        first_send((a, hf, 2), p.at[hf, a, near, :, two], r1.at[a, hf, 0, :, two], hf, 1)
+        first_send((a, hf, 3), p.at[hf, a, back, :, one], r1.at[a, hf, 1, :, one], hf, 3)
+
     for hf in range(2):
         d_copies[hf].wait_recv()
         own, his = (ut[k, hf].reshape(288, ROWS) for k in range(2))
         lhs = jnp.concatenate([own, own, his, his], axis=1)
         part = jnp.dot(lhs, dk[:, hf * HALF : (hf + 1) * HALF], preferred_element_type=F32)
         p[hf] = part.reshape(3, 4, 24, HALF)
-        q = mine[hf]
-        for a in range(3):
-            one, two = cut(a)
-            far, near, back = (q + 2) % 4, (q + 1) % 4, (q + 3) % 4
-            first_send((a, hf, 0), p.at[hf, a, far, :, one], r0.at[a, hf, :, one], hf, 1)
-            first_send((a, hf, 1), p.at[hf, a, far, :, two], r0.at[a, hf, :, two], hf, 3)
-            first_send((a, hf, 2), p.at[hf, a, near, :, two], r1.at[a, hf, 0, :, two], hf, 1)
-            first_send((a, hf, 3), p.at[hf, a, back, :, one], r1.at[a, hf, 1, :, one], hf, 3)
+        if hf == 0:
+            first(0, 0)
+    first(0, 1)
+    first(1, 0)
+    first(1, 1)
 
     def pass_on(a):
         one, two = cut(a)
@@ -296,35 +302,6 @@
             ones[a, hf, 1].wait_recv()
             f0[a, hf, :, two] = p[hf, a, back, :, two] + r0[a, hf, :, two]
             first_send((a, hf, 5), f0.at[a, hf, :, two], r1.at[a, hf, 1, :, two], hf, 3)
-
-    g = lax.dot_general(dk[0 : 2 * ROWS, :], wt[...], NT, preferred_element_type=F32)
-    pass_on(0)
-    g = g[0:ROWS] + g[ROWS : 2 * ROWS]
-    g = g[:, 512:768] + pltpu.roll(g[:, 256:512], ROWS - 1, axis=0) + pltpu.roll(g[:, 0:256], ROWS - 2, axis=0)
-    k = lax.broadcasted_iota(jnp.int32, (256, CH), 0)
-    chan = lax.broadcasted_iota(jnp.int32, (256, CH), 1)
-    spread = (chan == jnp.where(k < 128, 2 * k, 2 * (k - 128) + 1)).astype(F32).astype(BF16)
-    high = g.astype(BF16)
-    low = (g - high.astype(F32)).astype(BF16)
-    coarse = jnp.dot(jnp.concatenate([high, low], axis=0), spread, preferred_element_type=F32)
-    coarse = coarse[0:ROWS] + coarse[ROWS : 2 * ROWS]
-    pass_on(1)
-    grad_act = coarse * (sig * (1.0 + act * (1.0 - sig)))
-    gain_term = jnp.sum(grad_act * normed, axis=0, keepdims=True)
-    gh[ha] = jnp.concatenate([gain_term, jnp.zeros((1, 64), F32)], axis=1)
-
-    def gh_send(d, _):
-        remote(gh.at[ha], gh.at[ha], ghs.at[d - 1], ghr.at[d - 1], ((ha + d) % 16, wa, col)).start()
-        return 0
-
-    lax.fori_loop(1, 16, gh_send, 0)
-    pass_on(2)
-    grad_normed = grad_act * gain
-    grad_in = scale * (grad_normed - normed * jnp.mean(grad_normed * normed, axis=-1, keepdims=True))
-    for s in range(S):
-        gi_ref[:, s * CH : (s + 1) * CH] = grad_in[s * TP : s * TP + T].astype(BF16)
-    gi_out = pltpu.make_async_copy(gi_ref, gi_hbm, out_sem.at[0])
-    gi_out.start()
 
     twos = {}
 
@@ -409,25 +386,56 @@
         remote(gz.at[wa], gz.at[src], gzs.at[d - 1], gzr.at[d - 1], (ha, src, col)).wait_recv()
         return 0
 
+    g = lax.dot_general(dk[0 : 2 * ROWS, :], wt[...], NT, preferred_element_type=F32)
+    pass_on(0)
+    first(2, 0)
+    first(2, 1)
+    g = g[0:ROWS] + g[ROWS : 2 * ROWS]
+    g = g[:, 512:768] + pltpu.roll(g[:, 256:512], ROWS - 1, axis=0) + pltpu.roll(g[:, 0:256], ROWS - 2, axis=0)
+    k = lax.broadcasted_iota(jnp.int32, (256, CH), 0)
+    chan = lax.broadcasted_iota(jnp.int32, (256, CH), 1)
+    spread = (chan == jnp.where(k < 128, 2 * k, 2 * (k - 128) + 1)).astype(F32).astype(BF16)
+    high = g.astype(BF16)
+    low = (g - high.astype(F32)).astype(BF16)
+    coarse = jnp.dot(jnp.concatenate([high, low], axis=0), spread, preferred_element_type=F32)
+    coarse = coarse[0:ROWS] + coarse[ROWS : 2 * ROWS]
+    pass_on(1)
     second(0)
+    grad_act = coarse * (sig * (1.0 + act * (1.0 - sig)))
+    gain_term = jnp.sum(grad_act * normed, axis=0, keepdims=True)
+    gh[ha] = jnp.concatenate([gain_term, jnp.zeros((1, 64), F32)], axis=1)
+
+    def gh_send(d, _):
+        remote(gh.at[ha], gh.at[ha], ghs.at[d - 1], ghr.at[d - 1], ((ha + d) % 16, wa, col)).start()
+        return 0
+
+    lax.fori_loop(1, 16, gh_send, 0)
     second(1)
+    third(0)
+    pass_on(2)
+    grad_normed = grad_act * gain
+    grad_in = scale * (grad_normed - normed * jnp.mean(grad_normed * normed, axis=-1, keepdims=True))
+    for s in range(S):
+        gi_ref[:, s * CH : (s + 1) * CH] = grad_in[s * TP : s * TP + T].astype(BF16)
+    gi_out = pltpu.make_async_copy(gi_ref, gi_hbm, out_sem.at[0])
+    gi_out.start()
+
+    third(1)
+    second(2)
     lax.fori_loop(1, 16, gh_wait, 0)
     gz[wa] = jnp.sum(gh[...], axis=0)
     lax.fori_loop(1, 16, gz_send, 0)
-    third(0)
-    second(2)
-    third(1)
+    third(2)
+    finish(0)
     lax.fori_loop(1, 16, gz_wait, 0)
     gc[0] = jnp.sum(gz[...], axis=0)
     gc_copy = remote(gc.at[0], gc.at[1], gcs, gcr, (ha, wa, other))
     gc_copy.start()
-    third(2)
-    finish(0)
+    finish(1)
     gc_copy.wait()
     gg_ref[...] = (gc[0] + gc[1])[:, 0:CH]
     gg_out = pltpu.make_async_copy(gg_ref, gg_hbm, out_sem.at[1])
     gg_out.start()
-    finish(1)
     finish(2)
     gw_out = pltpu.make_async_copy(gw_ref, gw_hbm, out_sem.at[2])
     gw_out.start()

time: 58.7 us -> 59.6 us (1.015)
  Pallas kernels: 57.9 us -> 58.8 us
    pallas_call x1, Pallas kernels: 54.9 us -> 55.7 us  [on_device(): pl.pallas_call(kernel, out_shape=outs, in_specs=[hbm] * 5, out_specs=(hbm...]
where the time goes in v4:
time: 59.6 us; the launch traced here: 59.5 us
  Pallas kernels  58.8 us (99%)
  between operations  0.64 us (1%)
    pallas_call x1, Pallas kernels, on_device(): pl.pallas_call(kernel, out_shape=outs, in_specs=[hbm] * 5, out_specs=(hbm...  55.7 us
    pallas_call x1, Pallas kernels, on_device(): pl.pallas_call(hand_on, out_shape=outs, in_specs=[hbm] * 3, out_specs=(hb...  3.07 us

profile of v4, /device:TPU:6, one launch (start us, length us, event | category | flops | bytes accessed | tf_op | source)
XLA Modules:
  0.0 59.5 jit_solution(10098222023556989151)
XLA Ops:
  0.6 55.7 %shard_map.76 = (bf16[12,1536]{1,0:T(8,128)(2,1)}, f32[27,1,72]{2,1,0:T(1,128)}, f32[1,192]{1,0:T(1,128)}) custom-call(bf16[12,1536]{1,0:T(8,128)(2,1)} %bitcast.12, bf16[2,1536]{1,0:T(2,128)(2,1)} %bitcast.13, f32[1,192]{1,0:T(1,128)} %bitcast.14, bf16[27,36864]{1,0:T(8,128)(2,1)} %w_hbm.1, bf16[576,128]{1,0:T(8,128)(2,1)} %bitcast.11), custom_call_target="tpu_custom_call" | custom-call | tf_op jit(solution)/shard_map/pallas_call | solution.py:475
  56.4 3.1 %shard_map.77 = (bf16[12,1536]{1,0:T(8,128)(2,1)}, f32[27,1,72]{2,1,0:T(1,128)}, f32[1,192]{1,0:T(1,128)}) custom-call(bf16[12,1536]{1,0:T(8,128)(2,1)} %get-tuple-element.9.gi_from, f32[27,1,72]{2,1,0:T(1,128)} %get-tuple-element.10.gw_from, f32[1,192]{1,0:T(1,128)} %get-tuple-element.11.gg_from), custom_call_target="tpu_custom_call" | custom-call | tf_op jit(solution)/shard_map/pallas_call | solution.py:526

commit v5 on v3

--- a/solution.py
+++ b/solution.py
@@ -468,7 +468,7 @@
         kernel,
         out_shape=outs,
         in_specs=[hbm] * 5,
-        out_specs=(hbm, hbm, hbm),
+        out_specs=(pl.BlockSpec(memory_space=pltpu.VMEM),) * 3,
         scratch_shapes=[
             pltpu.VMEM((T, S * CH), BF16),
             pltpu.VMEM((27, 1, 72), F32),
@@ -506,7 +506,7 @@
             dma((3, 15)), dma((3, 15)), dma((15,)), dma((15,)), dma((15,)), dma((15,)), dma(()), dma(()),
         ],
         compiler_params=pltpu.CompilerParams(
-            collective_id=0, has_side_effects=True, vmem_limit_bytes=62 * 1024 * 1024
+            collective_id=0, has_side_effects=True, vmem_limit_bytes=(65536 - 10400) * 1024
         ),
     )(
         inputs.reshape(T, S * CH),
@@ -516,8 +516,8 @@
         cotangent.reshape(T, 2, 24, 128).transpose(0, 2, 1, 3).reshape(576, 128),
     )
     gi, gw, gg = pl.pallas_call(
-        hand_on, out_shape=outs, in_specs=[hbm] * 3, out_specs=(hbm, hbm, hbm), scratch_shapes=[dma((3,))],
-        compiler_params=pltpu.CompilerParams(vmem_limit_bytes=62 * 1024 * 1024),
+        hand_on, out_shape=outs, in_specs=[pl.BlockSpec(memory_space=pl.ANY)] * 3, out_specs=(hbm, hbm, hbm), scratch_shapes=[dma((3,))],
+        compiler_params=pltpu.CompilerParams(vmem_limit_bytes=16 * 1024 * 1024),
     )(*results)
     return gi.reshape(inputs.shape), gw.reshape(1, 27, 72), gg.reshape(CH)
 

time: 58.7 us -> 57.4 us (0.978)
  Pallas kernels: 57.9 us -> 55.2 us
  local copies, waits for them, and re-layouts: 0 us -> 1.36 us
    pallas_call x2, Pallas kernels: 57.9 us -> 55.2 us  [the longest x1 54.5 us: on_device(): pl.pallas_call(kernel, out_shape=outs, in_specs=[hbm] * 5, out_specs=(pl....]
    unnamed x0 -> x4, local copies, waits for them, and re-layouts: none -> 1.36 us
where the time goes in v5:
time: 57.4 us; the launch traced here: 57.2 us
  Pallas kernels  55.2 us (96%)
  local copies, waits for them, and re-layouts  1.36 us (2%)
  between operations  0.65 us (1%)
    pallas_call x1, Pallas kernels, on_device(): pl.pallas_call(kernel, out_shape=outs, in_specs=[hbm] * 5, out_specs=(pl....  54.5 us
    unnamed x4, local copies, waits for them, and re-layouts  1.36 us

profile of v5, /device:TPU:6, one launch (start us, length us, event | category | flops | bytes accessed | tf_op | source)
XLA Modules:
  0.0 57.2 jit_solution(14366841048408150954)
XLA Ops:
  0.6 0.0 copy-start
  0.6 0.7 %copy-done = bf16[1,2,1,1536]{3,1,2,0:T(2,128)(2,1)S(1)} copy-done((bf16[1,2,1,1536]{3,1,2,0:T(2,128)(2,1)S(1)}, bf16[1,2,1,1536]{3,1,2,0:T(2,128)(2,1)}, u32[]{:S(2)}) %copy-start) | copy-done | bytes 6168
  1.3 0.0 copy-start.1
  1.3 0.7 %copy-done.1 = f32[192]{0:T(256)S(1)} copy-done((f32[192]{0:T(256)S(1)}, f32[192]{0:T(256)}, u32[]{:S(2)}) %copy-start.1) | copy-done | bytes 792
  2.0 54.5 %shard_map.76 = (bf16[12,1536]{1,0:T(8,128)(2,1)S(1)}, f32[27,1,72]{2,1,0:T(1,128)S(1)}, f32[1,192]{1,0:T(1,128)S(1)}) custom-call(bf16[12,1536]{1,0:T(8,128)(2,1)} %bitcast.14, bf16[2,1536]{1,0:T(2,128)(2,1)S(1)} %bitcast.11, f32[1,192]{1,0:T(1,128)S(1)} %bitcast.12, bf16[27,36864]{1,0:T(8,128)(2,1)} %w_hbm.1, bf16[576,128]{1,0:T(8,128)(2,1)} %bitcast.13), custom_call_target="tpu_custom_call" | custom-call | tf_op jit(solution)/shard_map/pallas_call | solution.py:467
  56.5 0.7 %shard_map.77 = (bf16[12,1536]{1,0:T(8,128)(2,1)}, f32[27,1,72]{2,1,0:T(1,128)}, f32[1,192]{1,0:T(1,128)}) custom-call(bf16[12,1536]{1,0:T(8,128)(2,1)S(1)} %get-tuple-element.9.gi_from, f32[27,1,72]{2,1,0:T(1,128)S(1)} %get-tuple-element.10.gw_from, f32[1,192]{1,0:T(1,128)S(1)} %get-tuple-element.11.gg_from), custom_call_target="tpu_custom_call" | custom-call | tf_op jit(solution)/shard_map/pallas_call | solution.py:518
Async XLA Ops:
  0.6 0.7 %copy-start = (bf16[1,2,1,1536]{3,1,2,0:T(2,128)(2,1)S(1)}, bf16[1,2,1,1536]{3,1,2,0:T(2,128)(2,1)}, u32[]{:S(2)}) copy-start(bf16[1,2,1,1536]{3,1,2,0:T(2,128)(2,1)} %param.6) | copy-start | bytes 18436
  1.3 0.7 %copy-start.1 = (f32[192]{0:T(256)S(1)}, f32[192]{0:T(256)}, u32[]{:S(2)}) copy-start(f32[192]{0:T(256)} %param.7) | copy-start | bytes 2308
